TPU v7x, 256 devices: a whole 4x4x8 slice. The times are simulated.
256 devices in a mesh: inner: 16 (over z_hi, x, core), outer: 16 (over z_lo, y).
Axes of the slice: x: 4, y: 4, z: 8 (z_hi: 2, z_lo: 4; z = z_hi * 4 + z_lo), core: 2. Of those that a mesh axis runs over, the one named last changes fastest.
Arguments:
- queries: bfloat16 [98304, 1024], P(('inner', 'outer')), may hold values from -10 to 10
- key_rows: bfloat16 [98304, 1024], P(('inner', 'outer')), may hold values from -10 to 10
- value_rows: bfloat16 [98304, 1024], P(('inner', 'outer')), may hold values from -6 to 6
- cotangent: bfloat16 [98304, 1024], P(('inner', 'outer')), may hold values from -6 to 6
- page_mask: int32 [768, 3, 3], replicated, may hold values from 0 to 1, as said below
Outputs:
- grad_query: bfloat16 [98304, 1024], P(('inner', 'outer'))
- grad_key: bfloat16 [98304, 1024], P(('inner', 'outer'))
- grad_value: bfloat16 [98304, 1024], P(('inner', 'outer'))
Inputs may be any that keep to these rules, and one draw needn't show every extreme that they name: For query page p in block b = p // 3: page_mask[p, 0, p % 3] = 1 and page_mask[p, 0, j] = 0 for j > p % 3; page_mask[p, 1, :] is all zero when b % 16 == 0, and page_mask[p, 2, :] when b < 16.
All inputs are finite; a program needn't handle non-finite values.
Results may differ from a plain program's by a relative error of at most 0.0051.
Values may be sent and summed in bfloat16 or wider, within the bound.
No kernel may reach another device: no remote copies, remote signals or barrier semaphores. Data moves between devices by JAX's collectives and lax.ppermute only.
A program may use at most 192 MiB of HBM per device.

v0:
```python
import math

import jax
import jax.numpy as jnp
from jax import lax
from jax.sharding import PartitionSpec as P

HEADS = 8
HEAD_DIM = 128
PAGE = 128


NEG_FILL = -1e30


def from_behind(value, axis, steps):
    count = lax.axis_size(axis)
    initial, last = (max(0, -steps), min(count, count - steps))
    return lax.ppermute(value, axis, [(source, source + steps) for source in range(initial, last)])


def split_heads(matrix):
    return matrix.reshape(matrix.shape[0], HEADS, HEAD_DIM)


def block_mask(page_mask, block_at, source, tok_rows):
    page_count = tok_rows // PAGE
    picked = lax.dynamic_slice_in_dim(page_mask, block_at * page_count, page_count, 0)[:, source, :]
    expanded = jnp.broadcast_to(picked[:, None, :, None] > 0, (page_count, PAGE, page_count, PAGE))
    expanded = expanded.reshape(tok_rows, tok_rows)
    if source == 0:
        row_ids = lax.broadcasted_iota(jnp.int32, (tok_rows, tok_rows), 0)
        col_ids = lax.broadcasted_iota(jnp.int32, (tok_rows, tok_rows), 1)
        expanded = jnp.logical_and(expanded, col_ids <= row_ids)
    return expanded


def score_parts(queries, cotangent, key_rows, value_rows):
    scaling = 1.0 / math.sqrt(HEAD_DIM)
    scores = (
        jnp.einsum(
            "thd,shd->hts",
            split_heads(queries),
            split_heads(key_rows),
            preferred_element_type=jnp.float32,
        )
        * scaling
    )
    pushes = jnp.einsum(
        "thd,shd->hts",
        split_heads(cotangent),
        split_heads(value_rows),
        preferred_element_type=jnp.float32,
    )
    return (scores, pushes)


def pair_stats(queries, cotangent, key_rows, value_rows, allowed):
    scores, pushes = score_parts(queries, cotangent, key_rows, value_rows)
    nonempty = jnp.any(allowed, axis=1)
    row_max = jnp.max(jnp.where(allowed[None], scores, -jnp.inf), axis=2)
    row_max = jnp.where(nonempty[None], row_max, 0.0)
    weights = jnp.where(allowed[None], jnp.exp(scores - row_max[:, :, None]), 0.0)
    weight_sum = jnp.maximum(jnp.sum(weights, axis=2), 1.0)
    moment = jnp.sum(weights * pushes, axis=2)
    log_mass = jnp.where(nonempty[None], row_max + jnp.log(weight_sum), NEG_FILL)
    return ((log_mass, moment / weight_sum), (scores, pushes))


def combine_stats(first, second, third):
    highest = jnp.maximum(jnp.maximum(first[0], second[0]), third[0])
    factors = [jnp.exp(item[0] - highest) for item in (first, second, third)]
    mass_sum = factors[0] + factors[1] + factors[2]
    log_total = highest + jnp.log(mass_sum)
    correction = (factors[0] * first[1] + factors[1] * second[1] + factors[2] * third[1]) / mass_sum
    return (log_total, correction)


def pair_grads(queries, cotangent, key_rows, allowed, log_total, correction, scores, pushes):
    scaling = 1.0 / math.sqrt(HEAD_DIM)
    weighting = jnp.where(allowed[None], jnp.exp(scores - log_total[:, :, None]), 0.0)
    dscore = weighting * (pushes - correction[:, :, None])
    weight_low = weighting.astype(jnp.bfloat16)
    dscore_low = dscore.astype(jnp.bfloat16)
    feature_count = queries.shape[1]
    grad_v = jnp.einsum(
        "hts,thd->shd", weight_low, split_heads(cotangent), preferred_element_type=jnp.float32
    ).reshape(key_rows.shape[0], feature_count)
    grad_k = (
        jnp.einsum(
            "hts,thd->shd", dscore_low, split_heads(queries), preferred_element_type=jnp.float32
        ).reshape(key_rows.shape[0], feature_count)
        * scaling
    )
    grad_q = (
        jnp.einsum(
            "hts,shd->thd", dscore_low, split_heads(key_rows), preferred_element_type=jnp.float32
        ).reshape(queries.shape[0], feature_count)
        * scaling
    )
    return (grad_q, grad_k, grad_v)


def guarded(function, operands):
    return function(*operands)


def body(queries, key_rows, value_rows, cotangent, page_mask):
    tok_rows = queries.shape[0]
    inner_at = lax.axis_index("inner")
    outer_at = lax.axis_index("outer")
    outer_count = lax.axis_size("outer")
    block_at = inner_at * outer_count + outer_at
    own_mask = block_mask(page_mask, block_at, 0, tok_rows)
    own_stats, own_parts = pair_stats(queries, cotangent, key_rows, value_rows, own_mask)
    key_value = jnp.stack((key_rows, value_rows))
    near_values = from_behind(key_value, "outer", 1)
    far_values = from_behind(key_value, "inner", 1)
    near_mask = block_mask(page_mask, block_at, 1, tok_rows)
    far_mask = block_mask(page_mask, block_at, 2, tok_rows)
    near_stats, near_parts = guarded(
        pair_stats, (queries, cotangent, near_values[0], near_values[1], near_mask)
    )
    far_stats, far_parts = guarded(
        pair_stats, (queries, cotangent, far_values[0], far_values[1], far_mask)
    )
    log_total, correction = combine_stats(own_stats, near_stats, far_stats)
    own_grads = pair_grads(
        queries, cotangent, key_rows, own_mask, log_total, correction, own_parts[0], own_parts[1]
    )
    near_grads = guarded(
        pair_grads,
        (
            queries,
            cotangent,
            near_values[0],
            near_mask,
            log_total,
            correction,
            near_parts[0],
            near_parts[1],
        ),
    )
    far_grads = guarded(
        pair_grads,
        (
            queries,
            cotangent,
            far_values[0],
            far_mask,
            log_total,
            correction,
            far_parts[0],
            far_parts[1],
        ),
    )
    back_near = from_behind(jnp.stack((near_grads[1], near_grads[2])), "outer", -1)
    back_far = from_behind(jnp.stack((far_grads[1], far_grads[2])), "inner", -1)
    grad_q = own_grads[0] + near_grads[0] + far_grads[0]
    grad_k = own_grads[1] + back_near[0] + back_far[0]
    grad_v = own_grads[2] + back_near[1] + back_far[1]
    return (grad_q.astype(jnp.bfloat16), grad_k.astype(jnp.bfloat16), grad_v.astype(jnp.bfloat16))


def solution(mesh):
    in_specs = (
        P(("inner", "outer"), None),
        P(("inner", "outer"), None),
        P(("inner", "outer"), None),
        P(("inner", "outer"), None),
        P(),
    )
    out_specs = (
        P(("inner", "outer"), None),
        P(("inner", "outer"), None),
        P(("inner", "outer"), None),
    )
    return jax.shard_map(body, mesh=mesh, in_specs=in_specs, out_specs=out_specs, check_vma=False)
```

profile of v0, /device:TPU:152, one launch (start us, length us, event | category | flops | bytes accessed | tf_op | source)
XLA Modules:
  0.0 251.0 jit_solution(313491775085407616)
XLA Ops:
  0.6 1.5 copy.105
  2.1 1.8 copy.56
  3.9 1.3 pad_maximum_fusion.2
  5.3 1.9 collective-permute-start.1
  7.2 2.6 %collective-permute-start = (bf16[2,384,1024]{1,2,0:T(8,128)(2,1)}, bf16[2,384,1024]{1,2,0:T(8,128)(2,1)}, u32[]{:S(2)}, u32[]{:S(2)}) collective-permute-start(bf16[2,384,1024]{1,2,0:T(8,128)(2,1)} %pad_maximum_fusion.2), channel_id=1, source_target_pairs={{0,1},{1,2},{2,3},{3,4},{4,5},{5,6},{6,7},{7,8},{8,9},{9,10},{10,1... | collective-permute-start | bytes 4718600 | tf_op jit(solution)/shard_map/ppermute | solution.py:19
  9.8 0.8 dynamic-slice_compare_fusion.2
  11.4 0.4 copy.106
  11.7 7.6 %and_reduce_fusion = pred[3,128]{1,0:T(4,128)(4,1)S(1)} fusion(s32[3,128]{1,0:T(4,128)S(1)} %multiply_add_fusion, pred[3,3]{1,0:T(4,128)(4,1)S(1)} %bitcast.224), kind=kLoop, calls=%fused_computation.74 | loop fusion | flops 441984 | bytes 1929 | tf_op jit(solution)/shard_map/reduce_or | solution.py:60
  19.4 3.0 %select_reduce_fusion = (f32[8,384]{1,0:T(8,128)S(1)}, f32[8,384,384]{1,2,0:T(8,128)}) fusion(pred[384,384]{0,1:T(8,128)(4,1)S(1)} %copy.49, bf16[384,8,128]{0,2,1:T(8,128)(2,1)S(1)} %bitcast.183, bf16[384,8,128]{0,2,1:T(8,128)(2,1)S(1)} %bitcast.196), kind=kOutput, calls=%fused_computation.30 | convolution fusion | flops 305525760 | bytes 6451200 | tf_op jit(solution)/shard_map/thd,shd->hts/dot_general | solution.py:41
  22.4 7.0 %broadcast_reduce_fusion.1 = pred[3,128]{1,0:T(4,128)(4,1)S(1)} fusion(pred[3,3]{1,0:T(4,128)(4,1)S(1)} %bitcast.225), kind=kLoop, calls=%fused_computation.80 | loop fusion | flops 147072 | bytes 393 | tf_op jit(solution)/shard_map/reduce_or | solution.py:60
  29.8 0.3 copy.60
  30.4 0.3 copy.54
  30.7 1.5 copy.107
  32.2 7.0 %broadcast_reduce_fusion = pred[3,128]{1,0:T(4,128)(4,1)S(1)} fusion(pred[3,3]{1,0:T(4,128)(4,1)S(1)} %bitcast.228), kind=kLoop, calls=%fused_computation.79 | loop fusion | flops 147072 | bytes 393 | tf_op jit(solution)/shard_map/reduce_or | solution.py:60
  39.2 6.3 %fusion.16 = (f32[8,384]{1,0:T(8,128)S(1)}, f32[8,384]{1,0:T(8,128)S(1)}, f32[8,384,384]{1,2,0:T(8,128)}) fusion(f32[8,384,384]{1,2,0:T(8,128)} %get-tuple-element.30, f32[8,384]{1,0:T(8,128)S(1)} %broadcast_select_fusion.2, pred[384,384]{0,1:T(8,128)(4,1)S(1)} %copy.49, bf16[384,8,128]{0,2,1:T(8,128)(2,1)S(1)} %bitcast.189, ...), kind=kOutput, calls=%fused_computation.31 | convolution fusion | flops 309061632 | bytes 11194368 | tf_op jit(solution)/shard_map/thd,shd->hts/dot_general | solution.py:49
  45.5 0.6 collective-permute-done
  46.1 1.5 fusion.58
  47.6 0.9 fusion.11
  48.6 2.7 %fusion.57 = (bf16[1,384,1024]{1,2,0:T(8,128)(2,1)S(1)}, bf16[1,384,1024]{1,2,0:T(8,128)(2,1)S(1)}) fusion(bf16[2,384,1024]{1,2,0:T(8,128)(2,1)} %collective-permute-done.1), kind=kLoop, calls=%fused_computation.104 | loop fusion | bytes 3145728 | tf_op jit(solution)/shard_map/slice | solution.py:125
  51.3 0.9 fusion.6
  52.3 3.9 %fusion.19 = (f32[8,384]{1,0:T(8,128)S(1)}, f32[8,384]{1,0:T(8,128)S(1)}, f32[8,384,384]{2,1,0:T(8,128)}) fusion(f32[8,384,384]{2,1,0:T(8,128)S(1)} %get-tuple-element.33, f32[8,384]{1,0:T(8,128)S(1)} %broadcast_select_fusion.1, pred[384,384]{0,1:T(8,128)(4,1)S(1)} %copy.54, bf16[384,8,128]{0,2,1:T(8,128)(2,1)S(1)} %bitcast.206, ...), kind=kOutput, calls=%fused_computation.34 | convolution fusion | flops 309061632 | bytes 11194368 | tf_op jit(solution)/shard_map/thd,shd->hts/dot_general | solution.py:49
  56.2 3.8 %fusion.21 = (f32[8,384]{1,0:T(8,128)S(1)}, f32[8,384]{1,0:T(8,128)S(1)}, f32[8,384,384]{2,1,0:T(8,128)}) fusion(f32[8,384,384]{2,1,0:T(8,128)S(1)} %get-tuple-element.36, f32[8,384]{1,0:T(8,128)S(1)} %broadcast_select_fusion, pred[384,384]{0,1:T(8,128)(4,1)S(1)} %copy.60, bf16[384,8,128]{0,2,1:T(8,128)(2,1)S(1)} %bitcast.207, ...), kind=kOutput, calls=%fused_computation.36 | convolution fusion | flops 309061632 | bytes 11194368 | tf_op jit(solution)/shard_map/thd,shd->hts/dot_general | solution.py:49
  60.0 2.2 fusion.24
  62.3 2.2 fusion.22
  64.5 3.1 %copy.87 = f32[1,384,1024]{2,1,0:T(8,128)} copy(f32[1,384,1024]{1,2,0:T(8,128)} %bitcast.211) | data formatting | bytes 3145728 | tf_op jit(solution)/shard_map/stack;reshape | solution.py:158
  67.6 1.6 copy.80
  69.2 12.8 %fusion.2 = (bf16[8,384,384]{1,2,0:T(8,128)(2,1)S(1)}, bf16[8,384,384]{1,2,0:T(8,128)(2,1)S(1)}, bf16[8,384,384]{1,2,0:T(8,128)(2,1)}) fusion(f32[8,384,384]{2,1,0:T(8,128)} %get-tuple-element.37, f32[8,384,384]{2,1,0:T(8,128)} %copy-done.1, f32[8,384]{1,0:T(8,128)S(1)} %get-tuple-element.22, f32[8,384]{1,0:T(8,128)S(1)} %get-tuple-element.21, ...), kind=kLoop, calls=%fused_computation.4 | loop fusion | flops 21233664 | bytes 35856384 | tf_op jit(solution)/shard_map/convert_element_type | solution.py:84
  82.1 1.4 copy-done.5
  83.5 2.1 convolution_multiply_fusion.1
  85.5 3.0 %copy.79 = f32[1,384,1024]{2,1,0:T(8,128)} copy(f32[1,384,1024]{1,2,0:T(8,128)} %bitcast.203) | data formatting | bytes 3145728 | tf_op jit(solution)/shard_map/mul | solution.py:90
  88.6 2.0 convolution_multiply_fusion
  90.6 3.2 %copy.86 = f32[1,384,1024]{2,1,0:T(8,128)} copy(f32[1,384,1024]{1,2,0:T(8,128)} %bitcast.204) | data formatting | bytes 3145728 | tf_op jit(solution)/shard_map/mul | solution.py:90
  93.8 3.6 %pad_maximum_fusion.1 = f32[2,384,1024]{2,1,0:T(8,128)} fusion(f32[1,384,1024]{2,1,0:T(8,128)S(1)} %copy-done.14, f32[1,384,1024]{2,1,0:T(8,128)} %copy.86), kind=kLoop, calls=%fused_computation.38 | loop fusion | flops 786432 | bytes 6291456 | tf_op jit(solution)/shard_map/stack | solution.py:158
  97.4 19.3 %collective-permute-start.3 = (f32[2,384,1024]{2,1,0:T(8,128)}, f32[2,384,1024]{2,1,0:T(8,128)}, u32[]{:S(2)}, u32[]{:S(2)}) collective-permute-start(f32[2,384,1024]{2,1,0:T(8,128)} %pad_maximum_fusion.1), channel_id=1, source_target_pairs={{16,0},{32,16},{48,32},{64,48},{80,64},{96,80},{112,96},{128,112},... | collective-permute-start | bytes 9437192 | tf_op jit(solution)/shard_map/ppermute | solution.py:19
  116.7 3.3 %pad_maximum_fusion = f32[2,384,1024]{2,1,0:T(8,128)} fusion(f32[1,384,1024]{2,1,0:T(8,128)S(1)} %copy-done.13, f32[1,384,1024]{2,1,0:T(8,128)} %copy.79), kind=kLoop, calls=%fused_computation.37 | loop fusion | flops 786432 | bytes 6291456 | tf_op jit(solution)/shard_map/stack | solution.py:157
  120.0 1.9 collective-permute-start.2
  122.0 2.2 fusion.26
  124.2 3.2 %copy.90 = f32[384,1024]{1,0:T(8,128)} copy(f32[384,1024]{0,1:T(8,128)} %bitcast.209) | data formatting | bytes 3145728 | tf_op jit(solution)/shard_map/reshape | solution.py:88
  127.3 2.0 convolution_multiply_fusion.2
  129.3 3.0 %copy.81 = f32[384,1024]{1,0:T(8,128)} copy(f32[384,1024]{0,1:T(8,128)} %bitcast.202) | data formatting | bytes 3145728 | tf_op jit(solution)/shard_map/mul | solution.py:90
  132.4 2.7 %fusion.59 = f32[8,128,384]{2,1,0:T(8,128)S(1)} fusion(bf16[384,8,128]{0,2,1:T(8,128)(2,1)} %bitcast.199, bf16[8,384,384]{1,2,0:T(8,128)(2,1)} %copy-done.5), kind=kOutput, calls=%fused_computation.106 | convolution fusion | flops 301989888 | bytes 4718592 | tf_op jit(solution)/shard_map/hts,shd->thd/dot_general | solution.py:96
  135.1 0.7 fusion.60
  135.8 1.0 copy-done.3
  136.9 0.8 fusion.46
  137.7 1.2 copy.91
  138.8 12.9 %collective-permute-done.3 = f32[2,384,1024]{2,1,0:T(8,128)} collective-permute-done((f32[2,384,1024]{2,1,0:T(8,128)}, f32[2,384,1024]{2,1,0:T(8,128)}, u32[]{:S(2)}, u32[]{:S(2)}) %collective-permute-start.3) | collective-permute-done | bytes 3145760 | tf_op jit(solution)/shard_map/ppermute | solution.py:19
  151.7 93.5 %collective-permute-done.2 = f32[2,384,1024]{2,1,0:T(8,128)} collective-permute-done((f32[2,384,1024]{2,1,0:T(8,128)}, f32[2,384,1024]{2,1,0:T(8,128)}, u32[]{:S(2)}, u32[]{:S(2)}) %collective-permute-start.2) | collective-permute-done | bytes 3145760 | tf_op jit(solution)/shard_map/ppermute | solution.py:19
  245.2 5.3 %fusion.41 = (bf16[384,1024]{1,0:T(8,128)(2,1)}, bf16[384,1024]{1,0:T(8,128)(2,1)}) fusion(f32[2,384,1024]{2,1,0:T(8,128)} %collective-permute-done.3, f32[384,1024]{1,0:T(8,128)S(1)} %copy-done.15, f32[2,384,1024]{2,1,0:T(8,128)} %collective-permute-done.2, f32[384,1024]{1,0:T(8,128)} %copy.81), kind=kLoop, calls=%fused_computation.56 | loop fusion | flops 2359296 | bytes 11010048 | tf_op jit(solution)/shard_map/convert_element_type | solution.py:162
  (59 shorter events, 1.7 us)
Async XLA Ops:
  2.1 17.3 %copy-start.8 = (bf16[384,1024]{0,1:T(8,128)(2,1)}, bf16[384,1024]{0,1:T(8,128)(2,1)S(1)}, u32[]{:S(2)}) copy-start(bf16[384,1024]{0,1:T(8,128)(2,1)S(1)} %copy.105) | copy-start | bytes 2359300
  2.1 9.2 %copy-start.19 = (bf16[384,1024]{1,0:T(8,128)(2,1)S(1)}, bf16[384,1024]{1,0:T(8,128)(2,1)}, u32[]{:S(2)}) copy-start(bf16[384,1024]{1,0:T(8,128)(2,1)} %param.5) | copy-start | bytes 2359300
  5.3 43.4 %collective-permute-start.1 = (bf16[2,384,1024]{1,2,0:T(8,128)(2,1)}, bf16[2,384,1024]{1,2,0:T(8,128)(2,1)}, u32[]{:S(2)}, u32[]{:S(2)}) collective-permute-start(bf16[2,384,1024]{1,2,0:T(8,128)(2,1)} %pad_maximum_fusion.2), channel_id=1, source_target_pairs={{0,16},{16,32},{32,48},{48,64},{64,80},{80,96},{96,112},{112,128},... | collective-permute-start | bytes 4718600 | tf_op jit(solution)/shard_map/ppermute | solution.py:19
  7.2 38.9 %collective-permute-start = (bf16[2,384,1024]{1,2,0:T(8,128)(2,1)}, bf16[2,384,1024]{1,2,0:T(8,128)(2,1)}, u32[]{:S(2)}, u32[]{:S(2)}) collective-permute-start(bf16[2,384,1024]{1,2,0:T(8,128)(2,1)} %pad_maximum_fusion.2), channel_id=1, source_target_pairs={{0,1},{1,2},{2,3},{3,4},{4,5},{5,6},{6,7},{7,8},{8,9},{9,10},{10,1... | collective-permute-start | bytes 4718600 | tf_op jit(solution)/shard_map/ppermute | solution.py:19
  22.4 16.8 %copy-start.16 = (bf16[384,1024]{1,0:T(8,128)(2,1)S(1)}, bf16[384,1024]{1,0:T(8,128)(2,1)}, u32[]{:S(2)}) copy-start(bf16[384,1024]{1,0:T(8,128)(2,1)} %param.7) | copy-start | bytes 2359300
  30.7 29.4 %copy-start.17 = (pred[384,384]{0,1:T(8,128)(4,1)}, pred[384,384]{0,1:T(8,128)(4,1)S(1)}, u32[]{:S(2)}) copy-start(pred[384,384]{0,1:T(8,128)(4,1)S(1)} %copy.54) | copy-start | bytes 442372
  32.2 30.1 %copy-start.6 = (bf16[384,1024]{0,1:T(8,128)(2,1)}, bf16[384,1024]{0,1:T(8,128)(2,1)S(1)}, u32[]{:S(2)}) copy-start(bf16[384,1024]{0,1:T(8,128)(2,1)S(1)} %copy.107) | copy-start | bytes 2359300
  47.6 1.0 copy-start.10
  48.6 11.4 %copy-start = (f32[8,384,384]{2,1,0:T(8,128)}, f32[8,384,384]{2,1,0:T(8,128)S(1)}, u32[]{:S(2)}) copy-start(f32[8,384,384]{2,1,0:T(8,128)S(1)} %get-tuple-element.33) | copy-start | bytes 14155780
  51.3 1.0 copy-start.11
  52.3 10.0 %copy-start.1 = (f32[8,384,384]{2,1,0:T(8,128)}, f32[8,384,384]{2,1,0:T(8,128)S(1)}, u32[]{:S(2)}) copy-start(f32[8,384,384]{2,1,0:T(8,128)S(1)} %get-tuple-element.36) | copy-start | bytes 14155780
  64.5 3.2 %copy-start.18 = (f32[8,384,128]{1,2,0:T(8,128)S(1)}, f32[8,384,128]{1,2,0:T(8,128)}, u32[]{:S(2)}) copy-start(f32[8,384,128]{1,2,0:T(8,128)} %fusion.24) | copy-start | bytes 4718596
  82.1 1.4 copy-start.5
  82.1 6.5 %copy-start.2 = (bf16[8,384,384]{1,2,0:T(8,128)(2,1)}, bf16[8,384,384]{1,2,0:T(8,128)(2,1)S(1)}, u32[]{:S(2)}) copy-start(bf16[8,384,384]{1,2,0:T(8,128)(2,1)S(1)} %get-tuple-element.26) | copy-start | bytes 7077892
  90.6 3.2 %copy-start.14 = (f32[1,384,1024]{2,1,0:T(8,128)S(1)}, f32[1,384,1024]{2,1,0:T(8,128)}, u32[]{:S(2)}) copy-start(f32[1,384,1024]{2,1,0:T(8,128)} %copy.87) | copy-start | bytes 4718596
  90.6 31.4 %slice-start = ((s8[4718592]{0:T(1024)(128)(4,1)}), s8[524288]{0:T(1024)(128)(4,1)S(1)}, s32[]{:S(2)}) async-start(s8[4718592]{0:T(1024)(128)(4,1)} %bitcast.181), calls=%async_computation | async-start | bytes 1048576
  93.8 22.9 %copy-start.13 = (f32[1,384,1024]{2,1,0:T(8,128)S(1)}, f32[1,384,1024]{2,1,0:T(8,128)}, u32[]{:S(2)}) copy-start(f32[1,384,1024]{2,1,0:T(8,128)} %copy.80) | copy-start | bytes 4718596
  93.8 28.2 %slice-start.1 = ((s8[4718592]{0:T(1024)(128)(4,1)}), s8[4194304]{0:T(1024)(128)(4,1)S(1)}, s32[]{:S(2)}) async-start(s8[4718592]{0:T(1024)(128)(4,1)} %bitcast.181), calls=%async_computation.1 | async-start | bytes 8388608
  97.4 24.6 %copy-start.7 = (bf16[384,1024]{0,1:T(8,128)(2,1)S(1)}, bf16[384,1024]{0,1:T(8,128)(2,1)}, u32[]{:S(2)}) copy-start(bf16[384,1024]{0,1:T(8,128)(2,1)} %copy-done.6) | copy-start | bytes 2359300
  97.4 54.3 %collective-permute-start.3 = (f32[2,384,1024]{2,1,0:T(8,128)}, f32[2,384,1024]{2,1,0:T(8,128)}, u32[]{:S(2)}, u32[]{:S(2)}) collective-permute-start(f32[2,384,1024]{2,1,0:T(8,128)} %pad_maximum_fusion.1), channel_id=1, source_target_pairs={{16,0},{32,16},{48,32},{64,48},{80,64},{96,80},{112,96},{128,112},... | collective-permute-start | bytes 9437192 | tf_op jit(solution)/shard_map/ppermute | solution.py:19
  120.0 125.2 %collective-permute-start.2 = (f32[2,384,1024]{2,1,0:T(8,128)}, f32[2,384,1024]{2,1,0:T(8,128)}, u32[]{:S(2)}, u32[]{:S(2)}) collective-permute-start(f32[2,384,1024]{2,1,0:T(8,128)} %pad_maximum_fusion), channel_id=1, source_target_pairs={{1,0},{2,1},{3,2},{4,3},{5,4},{6,5},{7,6},{8,7},{9,8},{10,9},{11,1... | collective-permute-start | bytes 9437192 | tf_op jit(solution)/shard_map/ppermute | solution.py:19
  124.2 3.2 %copy-start.4 = (bf16[8,384,384]{1,2,0:T(8,128)(2,1)S(1)}, bf16[8,384,384]{1,2,0:T(8,128)(2,1)}, u32[]{:S(2)}) copy-start(bf16[8,384,384]{1,2,0:T(8,128)(2,1)} %get-tuple-element.28) | copy-start | bytes 7077892
  132.4 2.7 %copy-start.9 = (bf16[384,1024]{0,1:T(8,128)(2,1)S(1)}, bf16[384,1024]{0,1:T(8,128)(2,1)}, u32[]{:S(2)}) copy-start(bf16[384,1024]{0,1:T(8,128)(2,1)} %copy-done.8) | copy-start | bytes 2359300
  135.1 1.7 copy-start.3
  135.1 1.8 copy-start.12
  136.9 108.3 %copy-start.15 = (f32[384,1024]{1,0:T(8,128)S(1)}, f32[384,1024]{1,0:T(8,128)}, u32[]{:S(2)}) copy-start(f32[384,1024]{1,0:T(8,128)} %copy.90) | copy-start | bytes 4718596
where the time goes:
time: 256 us; the launch traced here: 251 us
  waiting for transfers between devices  107 us (42%)
  other arithmetic  49 us (19%)
  matrix products  35.6 us (14%)
  local copies, waits for them, and re-layouts  32.3 us (13%)
  starting transfers between devices  25.7 us (10%)
    ppermute x4, waiting for transfers between devices, from_behind(): lax.ppermute(value, axis, [(source, source + steps) for source in range(i...  107 us
    ppermute x4, starting transfers between devices, from_behind(): lax.ppermute(value, axis, [(source, source + steps) for source in range(i...  25.7 us
    reduce_or x3, other arithmetic, pair_stats(): nonempty = jnp.any(allowed, axis=1)  21.6 us
    dot_general x3, matrix products, score_parts(): jnp.einsum('thd,shd->hts', split_heads(cotangent), split_heads(value_rows...  13.9 us
    convert_element_type x1, other arithmetic, pair_grads(): dscore_low = dscore.astype(jnp.bfloat16)  12.8 us
    mul x3, local copies, waits for them, and re-layouts, pair_grads(): jnp.einsum('hts,thd->shd', dscore_low, split_heads(queries), preferred_el...  9.25 us
    dot_general x3, matrix products, pair_grads(): jnp.einsum('hts,thd->shd', weight_low, split_heads(cotangent), preferred_...  6.6 us
    dot_general x3, matrix products, pair_grads(): jnp.einsum('hts,thd->shd', dscore_low, split_heads(queries), preferred_el...  6.06 us
  transfers between devices with their start and end apart: 4, of which 3 were waited for; matrix products, arithmetic and copies ran while one was open for 23% of the time, Pallas kernels for 0%

commit v1 on v0

v1 whole, which is shorter than its diff:
```python
import functools
import math

import jax
import jax.numpy as jnp
from jax import lax
from jax.experimental import pallas as pl
from jax.experimental.pallas import tpu as pltpu
from jax.sharding import PartitionSpec as P

HEADS = 8
D = 128
PAGE = 128
PG = 3
TOK = PG * PAGE
AXES = ("inner", "outer")
MASKED = -1e30
SCALE = 1.0 / math.sqrt(D)
SCALE2 = SCALE * math.log2(math.e)
GROUPS = ((0, 4), (4, 4))
NT = (((1,), (1,)), ((), ()))
NN = (((1,), (0,)), ((), ()))
TN = (((0,), (0,)), ((), ()))


def dot(a, b, dims):
    return lax.dot_general(a, b, dims, preferred_element_type=jnp.float32)


def causal_bias():
    key_at = lax.broadcasted_iota(jnp.int32, (PAGE, PAGE), 0)
    query_at = lax.broadcasted_iota(jnp.int32, (PAGE, PAGE), 1)
    return jnp.where(key_at <= query_at, 0.0, MASKED).astype(jnp.float32)


def strips(keys, values, queries, cotangent, bias, own, causal):
    for j in range(PG):
        lo = j * PAGE if own else 0
        rows = slice(j * PAGE, (j + 1) * PAGE)
        scores = dot(keys[rows], queries[lo:], NT) * SCALE2 + bias[j : j + 1, lo:]
        if own:
            first = scores[:, :PAGE] + causal
            scores = first if j == PG - 1 else jnp.concatenate((first, scores[:, PAGE:]), axis=1)
        pushes = dot(values[rows], cotangent[lo:], NT)
        yield j, lo, scores, pushes


def stats_kernel(count, q, do, k, v, nk, nv, fk, fv, bias, out):
    h = pl.program_id(0)
    queries, cotangent = q[...], do[...]
    biases = bias[...]
    causal = causal_bias()
    parts = []
    for src, (keys, values) in enumerate(((k, v), (nk, nv), (fk, fv))):
        parts += list(
            strips(
                keys[...], values[...], queries, cotangent,
                biases[3 * src : 3 * src + 3], src == 0, causal,
            )
        )
    tops, sums, moments = [], [], []
    for i in range(PG):
        cols = slice(i * PAGE, (i + 1) * PAGE)
        here = [
            (s[:, i * PAGE - lo : (i + 1) * PAGE - lo], p[:, i * PAGE - lo : (i + 1) * PAGE - lo])
            for j, lo, s, p in parts
            if lo <= i * PAGE
        ]
        top = functools.reduce(jnp.maximum, [s for s, _ in here])
        top = jnp.max(top, axis=0, keepdims=True)
        mass, moment = 0.0, 0.0
        for s, p in here:
            e = jnp.exp2(s - top)
            mass = mass + e
            moment = moment + e * p
        mass = jnp.sum(mass, axis=0, keepdims=True)
        moment = jnp.sum(moment, axis=0, keepdims=True)
        rows = lax.broadcasted_iota(jnp.int32, (2 * count, PAGE), 0)
        held = jnp.where(rows == count + h, moment / mass, out[:, cols])
        out[:, cols] = jnp.where(rows == h, top + jnp.log2(mass), held)


def row_of(stats, at):
    rows = lax.broadcasted_iota(jnp.int32, stats.shape, 0)
    return jnp.sum(jnp.where(rows == at, stats, 0.0), axis=0, keepdims=True)


def weights(scores, pushes, total, correction):
    prob = jnp.exp2(scores - total)
    dscore = prob * (pushes - correction)
    return prob.astype(jnp.bfloat16), dscore.astype(jnp.bfloat16)


def query_kernel(count, q, do, k, v, nk, nv, fk, fv, bias, stats, *rest):
    dq_out, dk_out, dv_out = rest[-3:]
    h = pl.program_id(0)
    queries, cotangent = q[...], do[...]
    biases = bias[...]
    total, correction = row_of(stats[...], h), row_of(stats[...], count + h)
    causal = causal_bias()
    grad_q = jnp.zeros((TOK, D), jnp.float32)
    for src, (keys, values) in enumerate(((k, v), (nk, nv), (fk, fv))):
        own = src == 0
        parts = []
        for j, lo, s, p in strips(
            keys[...], values[...], queries, cotangent, biases[3 * src : 3 * src + 3], own, causal
        ):
            prob, dscore = weights(s, p, total[:, lo:], correction[:, lo:])
            if own:
                rows = slice(j * PAGE, (j + 1) * PAGE)
                dv_out[rows] = dot(prob, cotangent[lo:], NN)
                dk_out[rows] = dot(dscore, queries[lo:], NN)
            if lo:
                dscore = jnp.concatenate((jnp.zeros((PAGE, lo), dscore.dtype), dscore), axis=1)
            parts.append(dscore)
        grad_q = grad_q + dot(jnp.concatenate(parts, axis=0), keys[...], TN)
    dq_out[...] = (grad_q * SCALE).astype(dq_out.dtype)


def key_kernel(count, k, v, own_dk, own_dv, nq, ndo, nstats, fq, fdo, fstats, bias, *rest):
    dk_out, dv_out = rest[-2:]
    h = pl.program_id(0)
    keys, values = k[...], v[...]
    biases = bias[...]
    lines = [
        (row_of(st[...], h), row_of(st[...], count + h)) for st in (nstats, fstats)
    ]
    for j in range(PG):
        rows = slice(j * PAGE, (j + 1) * PAGE)
        grad_k, grad_v = own_dk[rows], own_dv[rows]
        for src, (q, do) in enumerate(((nq, ndo), (fq, fdo))):
            queries, cotangent = q[...], do[...]
            at = 9 + 3 * src + j
            s = dot(keys[rows], queries, NT) * SCALE2 + biases[at : at + 1]
            p = dot(values[rows], cotangent, NT)
            prob, dscore = weights(s, p, *lines[src])
            grad_v = grad_v + dot(prob, cotangent, NN)
            grad_k = grad_k + dot(dscore, queries, NN)
        dk_out[rows] = (grad_k * SCALE).astype(dk_out.dtype)
        dv_out[rows] = grad_v.astype(dv_out.dtype)


def column(offset):
    return pl.BlockSpec((TOK, D), lambda h: (0, h + offset))


def whole(shape):
    return pl.BlockSpec(shape, lambda h: (0, 0))


def call(kernel, name, count, ins, outs, carried, pairs, dots):
    arrays = [a for a, _ in ins]
    in_specs = [s for _, s in ins]
    aliases = {}
    for at, array in enumerate(carried):
        aliases[len(arrays)] = at
        arrays.append(array)
        in_specs.append(pl.BlockSpec(memory_space=pl.ANY))
    return pl.pallas_call(
        functools.partial(kernel, count),
        name=name,
        grid=(count,),
        in_specs=in_specs,
        out_specs=[s for _, s in outs],
        out_shape=[s for s, _ in outs],
        input_output_aliases=aliases,
        compiler_params=pltpu.CompilerParams(
            dimension_semantics=("arbitrary",), vmem_limit_bytes=48 * 1024 * 1024
        ),
        cost_estimate=pl.CostEstimate(
            flops=2 * dots * count * TOK * TOK * D,
            bytes_accessed=len(ins) * count * TOK * D * 2,
            transcendentals=pairs * count * TOK * TOK,
        ),
    )(*arrays)


def biases_of(page_mask, block_at, block_count):
    flat = page_mask.reshape(block_count, PG, 3, PG)

    def picked(at, source):
        part = lax.dynamic_slice(
            flat, (jnp.minimum(at, block_count - 1), 0, source, 0), (1, PG, 1, PG)
        )
        inside = at < block_count
        part = jnp.where(inside, part.reshape(PG, PG).T, 0)
        return jnp.where(part > 0, 0.0, MASKED).astype(jnp.float32)

    rows = [picked(block_at, source) for source in range(3)]
    rows += [picked(block_at + 1, 1), picked(block_at + lax.axis_size("outer"), 2)]
    rows = jnp.concatenate(rows + [jnp.zeros((1, PG), jnp.float32)], axis=0)
    return jnp.broadcast_to(rows[:, :, None], (16, PG, PAGE)).reshape(16, TOK)


def body(queries, key_rows, value_rows, cotangent, page_mask):
    n_inner, n_outer = lax.axis_size("inner"), lax.axis_size("outer")
    block_at = lax.axis_index("inner") * n_outer + lax.axis_index("outer")
    near = [
        (i * n_outer + o, i * n_outer + o + 1) for i in range(n_inner) for o in range(n_outer - 1)
    ]
    far = [
        (i * n_outer + o, (i + 1) * n_outer + o) for i in range(n_inner - 1) for o in range(n_outer)
    ]
    near_back, far_back = [(b, a) for a, b in near], [(b, a) for a, b in far]

    def send(array, pairs):
        return lax.ppermute(array, AXES, pairs)

    moved = []
    for first, count in GROUPS:
        cols = slice(first * D, (first + count) * D)
        key_value = jnp.concatenate((key_rows[:, cols], value_rows[:, cols]), axis=1)
        query_cot = jnp.concatenate((queries[:, cols], cotangent[:, cols]), axis=1)
        moved.append(
            (
                send(key_value, near),
                send(query_cot, near_back),
                send(key_value, far),
                send(query_cot, far_back),
            )
        )
    bias = biases_of(page_mask, block_at, n_inner * n_outer)

    out = jax.ShapeDtypeStruct((TOK, HEADS * D), jnp.bfloat16)
    grad_q, grad_k, grad_v = None, None, None
    for (first, count), (near_kv, near_qc, far_kv, far_qc) in zip(GROUPS, moved):
        local = column(first)
        query_side = [
            (queries, local),
            (cotangent, local),
            (key_rows, local),
            (value_rows, local),
            (near_kv, column(0)),
            (near_kv, column(count)),
            (far_kv, column(0)),
            (far_kv, column(count)),
            (bias, whole((16, TOK))),
        ]
        stat_block = whole((2 * count, TOK))
        stat_shape = jax.ShapeDtypeStruct((2 * count, TOK), jnp.float32)
        (stats,) = call(
            stats_kernel, "stats", count, query_side, [(stat_shape, stat_block)], [], 3, 6
        )
        near_stats = send(stats, near_back)
        far_stats = send(stats, far_back)
        part = jax.ShapeDtypeStruct((TOK, count * D), jnp.float32)
        grad_q, own_dk, own_dv = call(
            query_kernel, "query_side", count,
            query_side + [(stats, stat_block)],
            [(out, local), (part, column(0)), (part, column(0))],
            [] if grad_q is None else [grad_q], 3, 11,
        )
        grad_k, grad_v = call(
            key_kernel, "key_side", count,
            [
                (key_rows, local),
                (value_rows, local),
                (own_dk, column(0)),
                (own_dv, column(0)),
                (near_qc, column(0)),
                (near_qc, column(count)),
                (near_stats, stat_block),
                (far_qc, column(0)),
                (far_qc, column(count)),
                (far_stats, stat_block),
                (bias, whole((16, TOK))),
            ],
            [(out, local), (out, local)],
            [] if grad_k is None else [grad_k, grad_v], 2, 8,
        )
    return (grad_q, grad_k, grad_v)


def solution(mesh):
    split = P(AXES, None)
    return jax.shard_map(
        body, mesh=mesh, in_specs=(split, split, split, split, P()),
        out_specs=(split, split, split), check_vma=False,
    )
```

time: 256 us -> 135 us (0.53)
  the two profiles are of different devices: /device:TPU:152 before, /device:TPU:241 now
where the time goes in v1:
time: 135 us; the launch traced here: 134 us
  starting transfers between devices  62.1 us (46%)
  Pallas kernels  44.7 us (33%)
  waiting for transfers between devices  13.7 us (10%)
  local copies, waits for them, and re-layouts  8.35 us (6%)
  other arithmetic  3.85 us (3%)
    ppermute x12, starting transfers between devices, send(): return lax.ppermute(array, AXES, pairs)  62.1 us
    pallas_call x6, Pallas kernels, call(): pl.pallas_call(functools.partial(kernel, count), name=name, grid=(count,)...  44.7 us
    ppermute x12, waiting for transfers between devices, send(): return lax.ppermute(array, AXES, pairs)  13.7 us
    unnamed x25, local copies, waits for them, and re-layouts  4.07 us
  transfers between devices with their start and end apart: 12, of which 2 were waited for; matrix products, arithmetic and copies ran while one was open for 5% of the time, Pallas kernels for 28%

profile of v1, /device:TPU:241, one launch (start us, length us, event | category | flops | bytes accessed | tf_op | source)
XLA Modules:
  0.0 133.7 jit_solution(10039915392409244408)
XLA Ops:
  0.6 1.5 %fusion.2 = (bf16[384,512]{1,0:T(8,128)(2,1)S(1)}, bf16[384,512]{1,0:T(8,128)(2,1)S(1)}, bf16[384,512]{1,0:T(8,128)(2,1)S(1)}, bf16[384,512]{1,0:T(8,128)(2,1)S(1)}) fusion(bf16[384,1024]{1,0:T(8,128)(2,1)} %k.11, bf16[384,1024]{1,0:T(8,128)(2,1)} %v.11), kind=kLoop, calls=%fused_computation.17 | loop fusion | bytes 3145728 | tf_op jit(solution)/shard_map/slice | solution.py:212
  2.1 0.1 pad_maximum_fusion.1
  2.2 0.0 copy-start.2
  2.2 0.0 copy-start.3
  2.2 3.0 %collective-permute-start.2 = (bf16[384,1024]{1,0:T(8,128)(2,1)S(1)}, bf16[384,1024]{1,0:T(8,128)(2,1)S(1)}, u32[]{:S(2)}, u32[]{:S(2)}) collective-permute-start(bf16[384,1024]{1,0:T(8,128)(2,1)S(1)} %pad_maximum_fusion.1), channel_id=1, source_target_pairs={{0,1},{1,2},{2,3},{3,4},{4,5},{5,6},{6,7},{7,8},{8,9},{9,10},{10,1... | collective-permute-start | bytes 2359304 | tf_op jit(solution)/shard_map/ppermute | solution.py:207
  5.3 4.0 %collective-permute-start.3 = (bf16[384,1024]{1,0:T(8,128)(2,1)S(1)}, bf16[384,1024]{1,0:T(8,128)(2,1)S(1)}, u32[]{:S(2)}, u32[]{:S(2)}) collective-permute-start(bf16[384,1024]{1,0:T(8,128)(2,1)S(1)} %pad_maximum_fusion.1), channel_id=1, source_target_pairs={{0,16},{1,17},{2,18},{3,19},{4,20},{5,21},{6,22},{7,23},{8,24},{9,... | collective-permute-start | bytes 2359304 | tf_op jit(solution)/shard_map/ppermute | solution.py:207
  9.2 1.0 pad_maximum_fusion
  10.2 1.9 %collective-permute-start = (bf16[384,1024]{1,0:T(8,128)(2,1)}, bf16[384,1024]{1,0:T(8,128)(2,1)S(1)}, u32[]{:S(2)}, u32[]{:S(2)}) collective-permute-start(bf16[384,1024]{1,0:T(8,128)(2,1)} %pad_maximum_fusion), channel_id=1, source_target_pairs={{0,1},{1,2},{2,3},{3,4},{4,5},{5,6},{6,7},{7,8},{8,9},{9,10},{10,1... | collective-permute-start | bytes 2359304 | tf_op jit(solution)/shard_map/ppermute | solution.py:207
  12.1 1.9 %collective-permute-start.1 = (bf16[384,1024]{1,0:T(8,128)(2,1)}, bf16[384,1024]{1,0:T(8,128)(2,1)}, u32[]{:S(2)}, u32[]{:S(2)}) collective-permute-start(bf16[384,1024]{1,0:T(8,128)(2,1)} %pad_maximum_fusion), channel_id=1, source_target_pairs={{0,16},{1,17},{2,18},{3,19},{4,20},{5,21},{6,22},{7,23},{8,24},{9,... | collective-permute-start | bytes 2359304 | tf_op jit(solution)/shard_map/ppermute | solution.py:207
  14.1 0.1 fusion
  14.2 1.0 pad_maximum_fusion.3
  15.2 2.5 %collective-permute-start.10 = (bf16[384,1024]{1,0:T(8,128)(2,1)}, bf16[384,1024]{1,0:T(8,128)(2,1)}, u32[]{:S(2)}, u32[]{:S(2)}) collective-permute-start(bf16[384,1024]{1,0:T(8,128)(2,1)} %pad_maximum_fusion.3), channel_id=1, source_target_pairs={{16,0},{17,1},{18,2},{19,3},{20,4},{21,5},{22,6},{23,7},{24,8},{25... | collective-permute-start | bytes 2359304 | tf_op jit(solution)/shard_map/ppermute | solution.py:207
  17.7 4.9 %collective-permute-done.2.nk.nv = bf16[384,1024]{1,0:T(8,128)(2,1)S(1)} collective-permute-done((bf16[384,1024]{1,0:T(8,128)(2,1)S(1)}, bf16[384,1024]{1,0:T(8,128)(2,1)S(1)}, u32[]{:S(2)}, u32[]{:S(2)}) %collective-permute-start.2) | collective-permute-done | bytes 786464 | tf_op jit(solution)/shard_map/ppermute | solution.py:207
  22.6 2.1 %collective-permute-start.8 = (bf16[384,1024]{1,0:T(8,128)(2,1)}, bf16[384,1024]{1,0:T(8,128)(2,1)}, u32[]{:S(2)}, u32[]{:S(2)}) collective-permute-start(bf16[384,1024]{1,0:T(8,128)(2,1)} %pad_maximum_fusion.3), channel_id=1, source_target_pairs={{1,0},{2,1},{3,2},{4,3},{5,4},{6,5},{7,6},{8,7},{9,8},{10,9},{11,1... | collective-permute-start | bytes 2359304 | tf_op jit(solution)/shard_map/ppermute | solution.py:207
  24.7 0.0 copy-start
  24.7 0.0 copy-start.1
  24.7 1.0 pad_maximum_fusion.2
  25.7 0.9 copy-done.9
  26.6 4.2 %collective-permute-start.4 = (bf16[384,1024]{1,0:T(8,128)(2,1)}, bf16[384,1024]{1,0:T(8,128)(2,1)}, u32[]{:S(2)}, u32[]{:S(2)}) collective-permute-start(bf16[384,1024]{1,0:T(8,128)(2,1)} %pad_maximum_fusion.2), channel_id=1, source_target_pairs={{1,0},{2,1},{3,2},{4,3},{5,4},{6,5},{7,6},{8,7},{9,8},{10,9},{11,1... | collective-permute-start | bytes 2359304 | tf_op jit(solution)/shard_map/ppermute | solution.py:207
  30.8 8.8 %collective-permute-done.nk.nv = bf16[384,1024]{1,0:T(8,128)(2,1)S(1)} collective-permute-done((bf16[384,1024]{1,0:T(8,128)(2,1)}, bf16[384,1024]{1,0:T(8,128)(2,1)S(1)}, u32[]{:S(2)}, u32[]{:S(2)}) %collective-permute-start) | collective-permute-done | bytes 786464 | tf_op jit(solution)/shard_map/ppermute | solution.py:207
  39.6 0.9 copy-done.4
  40.5 3.3 %collective-permute-start.6 = (bf16[384,1024]{1,0:T(8,128)(2,1)}, bf16[384,1024]{1,0:T(8,128)(2,1)}, u32[]{:S(2)}, u32[]{:S(2)}) collective-permute-start(bf16[384,1024]{1,0:T(8,128)(2,1)} %pad_maximum_fusion.2), channel_id=1, source_target_pairs={{16,0},{17,1},{18,2},{19,3},{20,4},{21,5},{22,6},{23,7},{24,8},{25... | collective-permute-start | bytes 2359304 | tf_op jit(solution)/shard_map/ppermute | solution.py:207
  43.9 2.0 %reshape.58 = s32[256,3,3,3]{1,0,3,2:T(8,128)} reshape(s32[768,3,3]{0,2,1:T(4,128)S(1)} %copy-done.11) | data formatting | bytes 55296 | tf_op jit(solution)/shard_map/reshape | solution.py:179
  45.8 0.8 compare_select_fusion
  46.7 0.1 copy.17
  46.7 0.1 copy.18
  46.8 0.1 copy.19
  46.9 0.1 copy.20
  47.0 0.1 copy.21
  47.1 0.1 concatenate.16
  47.2 0.1 copy.22
  47.3 0.1 broadcast_in_dim.33
  47.4 0.0 copy-start.7
  47.4 1.1 copy-done.7
  48.5 1.1 copy-done.10
  49.7 5.1 %stats.3 = f32[8,384]{1,0:T(8,128)S(1)} custom-call(bf16[384,1024]{1,0:T(8,128)(2,1)S(1)} %copy-done.2, bf16[384,1024]{1,0:T(8,128)(2,1)S(1)} %copy-done.3, bf16[384,1024]{1,0:T(8,128)(2,1)S(1)} %copy-done, bf16[384,1024]{1,0:T(8,128)(2,1)S(1)} %copy-done.1, bf16[384,1024]{1,0:T(8,128)(2,1)S(1)} %copy-done.7, bf16[384,1024]{1,0:T(8,128)(2,1)S(1)} %copy-done.7, ...), custom_call_target="tpu_custom_call" | custom-call | flops 905969664 | bytes 3538944 | tf_op jit(solution)/shard_map/stats/pallas_call | solution.py:159
  54.8 0.0 copy-start.8
  54.8 0.0 collective-permute-done.1.fk.fv
  54.8 4.3 %collective-permute-start.11 = (f32[8,384]{1,0:T(8,128)S(1)}, f32[8,384]{1,0:T(8,128)S(1)}, u32[]{:S(2)}, u32[]{:S(2)}) collective-permute-start(f32[8,384]{1,0:T(8,128)S(1)} %stats.3), channel_id=1, source_target_pairs={{16,0},{17,1},{18,2},{19,3},{20,4},{21,5},{22,6},{23,7},{24,8},{25... | collective-permute-start | bytes 36872 | tf_op jit(solution)/shard_map/ppermute | solution.py:207
  59.1 5.7 %stats.2 = f32[8,384]{1,0:T(8,128)S(1)} custom-call(bf16[384,1024]{1,0:T(8,128)(2,1)S(1)} %copy-done.2, bf16[384,1024]{1,0:T(8,128)(2,1)S(1)} %copy-done.3, bf16[384,1024]{1,0:T(8,128)(2,1)S(1)} %copy-done, bf16[384,1024]{1,0:T(8,128)(2,1)S(1)} %copy-done.1, bf16[384,1024]{1,0:T(8,128)(2,1)S(1)} %copy-done.5, bf16[384,1024]{1,0:T(8,128)(2,1)S(1)} %copy-done.5, ...), custom_call_target="tpu_custom_call" | custom-call | flops 905969664 | bytes 3538944 | tf_op jit(solution)/shard_map/stats/pallas_call | solution.py:159
  64.9 9.1 %query_side.2 = (bf16[384,1024]{1,0:T(8,128)(2,1)}, f32[384,512]{1,0:T(8,128)S(1)}, f32[384,512]{1,0:T(8,128)S(1)}) custom-call(bf16[384,1024]{1,0:T(8,128)(2,1)S(1)} %copy-done.2, bf16[384,1024]{1,0:T(8,128)(2,1)S(1)} %copy-done.3, bf16[384,1024]{1,0:T(8,128)(2,1)S(1)} %copy-done, bf16[384,1024]{1,0:T(8,128)(2,1)S(1)} %copy-done.1, ...), custom_call_target="tpu_custom_call" | custom-call | flops 1660944384 | bytes 3932160 | tf_op jit(solution)/shard_map/query_side/pallas_call | solution.py:159
  74.0 0.0 collective-permute-done.10.fq.fdo
  74.0 2.1 %collective-permute-start.9 = (f32[8,384]{1,0:T(8,128)S(1)}, f32[8,384]{1,0:T(8,128)S(1)}, u32[]{:S(2)}, u32[]{:S(2)}) collective-permute-start(f32[8,384]{1,0:T(8,128)S(1)} %stats.3), channel_id=1, source_target_pairs={{1,0},{2,1},{3,2},{4,3},{5,4},{6,5},{7,6},{8,7},{9,8},{10,9},{11,1... | collective-permute-start | bytes 36872 | tf_op jit(solution)/shard_map/ppermute | solution.py:207
  76.1 9.1 %query_side.3 = (bf16[384,1024]{1,0:T(8,128)(2,1)}, f32[384,512]{1,0:T(8,128)S(1)}, f32[384,512]{1,0:T(8,128)S(1)}) custom-call(bf16[384,1024]{1,0:T(8,128)(2,1)S(1)} %copy-done.2, bf16[384,1024]{1,0:T(8,128)(2,1)S(1)} %copy-done.3, bf16[384,1024]{1,0:T(8,128)(2,1)S(1)} %copy-done, ...), custom_call_target="tpu_custom_call", output_to_operand_aliasing={{0}: (10, {})} | custom-call | flops 1660944384 | bytes 3932160 | tf_op jit(solution)/shard_map/query_side/pallas_call | solution.py:159
  85.2 30.2 %collective-permute-start.5 = (f32[8,384]{1,0:T(8,128)S(1)}, f32[8,384]{1,0:T(8,128)S(1)}, u32[]{:S(2)}, u32[]{:S(2)}) collective-permute-start(f32[8,384]{1,0:T(8,128)S(1)} %stats.2), channel_id=1, source_target_pairs={{1,0},{2,1},{3,2},{4,3},{5,4},{6,5},{7,6},{8,7},{9,8},{10,9},{11,1... | collective-permute-start | bytes 36872 | tf_op jit(solution)/shard_map/ppermute | solution.py:207
  115.4 2.5 %collective-permute-start.7 = (f32[8,384]{1,0:T(8,128)S(1)}, f32[8,384]{1,0:T(8,128)S(1)}, u32[]{:S(2)}, u32[]{:S(2)}) collective-permute-start(f32[8,384]{1,0:T(8,128)S(1)} %stats.2), channel_id=1, source_target_pairs={{16,0},{17,1},{18,2},{19,3},{20,4},{21,5},{22,6},{23,7},{24,8},{25... | collective-permute-start | bytes 36872 | tf_op jit(solution)/shard_map/ppermute | solution.py:207
  117.9 7.9 %key_side.2 = (bf16[384,1024]{1,0:T(8,128)(2,1)}, bf16[384,1024]{1,0:T(8,128)(2,1)}) custom-call(bf16[384,1024]{1,0:T(8,128)(2,1)S(1)} %copy-done, bf16[384,1024]{1,0:T(8,128)(2,1)S(1)} %copy-done.1, f32[384,512]{1,0:T(8,128)S(1)} %get-tuple-element.17.own_dk, f32[384,512]{1,0:T(8,128)S(1)} %get-tuple-element.18.own_dv, ...), custom_call_target="tpu_custom_call" | custom-call | flops 1207959552 | bytes 4325376 | tf_op jit(solution)/shard_map/key_side/pallas_call | solution.py:159
  125.8 7.9 %key_side.3 = (bf16[384,1024]{1,0:T(8,128)(2,1)}, bf16[384,1024]{1,0:T(8,128)(2,1)}) custom-call(bf16[384,1024]{1,0:T(8,128)(2,1)S(1)} %copy-done, bf16[384,1024]{1,0:T(8,128)(2,1)S(1)} %copy-done.1, f32[384,512]{1,0:T(8,128)S(1)} %get-tuple-element.15.own_dk, ...), custom_call_target="tpu_custom_call", output_to_operand_aliasing={{0}: (11, {}), {1}: (12, {})} | custom-call | flops 1207959552 | bytes 4325376 | tf_op jit(solution)/shard_map/key_side/pallas_call | solution.py:159
  (24 shorter events, 0.1 us)
Async XLA Ops:
  2.2 11.9 %copy-start.2 = (bf16[384,1024]{1,0:T(8,128)(2,1)S(1)}, bf16[384,1024]{1,0:T(8,128)(2,1)}, u32[]{:S(2)}) copy-start(bf16[384,1024]{1,0:T(8,128)(2,1)} %q.7) | copy-start | bytes 2359300
  2.2 11.9 %copy-start.3 = (bf16[384,1024]{1,0:T(8,128)(2,1)S(1)}, bf16[384,1024]{1,0:T(8,128)(2,1)}, u32[]{:S(2)}) copy-start(bf16[384,1024]{1,0:T(8,128)(2,1)} %do.7) | copy-start | bytes 2359300
  2.2 20.4 %collective-permute-start.2 = (bf16[384,1024]{1,0:T(8,128)(2,1)S(1)}, bf16[384,1024]{1,0:T(8,128)(2,1)S(1)}, u32[]{:S(2)}, u32[]{:S(2)}) collective-permute-start(bf16[384,1024]{1,0:T(8,128)(2,1)S(1)} %pad_maximum_fusion.1), channel_id=1, source_target_pairs={{0,1},{1,2},{2,3},{3,4},{4,5},{5,6},{6,7},{7,8},{8,9},{9,10},{10,1... | collective-permute-start | bytes 2359304 | tf_op jit(solution)/shard_map/ppermute | solution.py:207
  5.3 20.5 %collective-permute-start.3 = (bf16[384,1024]{1,0:T(8,128)(2,1)S(1)}, bf16[384,1024]{1,0:T(8,128)(2,1)S(1)}, u32[]{:S(2)}, u32[]{:S(2)}) collective-permute-start(bf16[384,1024]{1,0:T(8,128)(2,1)S(1)} %pad_maximum_fusion.1), channel_id=1, source_target_pairs={{0,16},{1,17},{2,18},{3,19},{4,20},{5,21},{6,22},{7,23},{8,24},{9,... | collective-permute-start | bytes 2359304 | tf_op jit(solution)/shard_map/ppermute | solution.py:207
  10.2 29.4 %collective-permute-start = (bf16[384,1024]{1,0:T(8,128)(2,1)}, bf16[384,1024]{1,0:T(8,128)(2,1)S(1)}, u32[]{:S(2)}, u32[]{:S(2)}) collective-permute-start(bf16[384,1024]{1,0:T(8,128)(2,1)} %pad_maximum_fusion), channel_id=1, source_target_pairs={{0,1},{1,2},{2,3},{3,4},{4,5},{5,6},{6,7},{7,8},{8,9},{9,10},{10,1... | collective-permute-start | bytes 2359304 | tf_op jit(solution)/shard_map/ppermute | solution.py:207
  12.1 42.6 %collective-permute-start.1 = (bf16[384,1024]{1,0:T(8,128)(2,1)}, bf16[384,1024]{1,0:T(8,128)(2,1)}, u32[]{:S(2)}, u32[]{:S(2)}) collective-permute-start(bf16[384,1024]{1,0:T(8,128)(2,1)} %pad_maximum_fusion), channel_id=1, source_target_pairs={{0,16},{1,17},{2,18},{3,19},{4,20},{5,21},{6,22},{7,23},{8,24},{9,... | collective-permute-start | bytes 2359304 | tf_op jit(solution)/shard_map/ppermute | solution.py:207
  15.2 28.7 %copy-start.11 = (s32[768,3,3]{0,2,1:T(4,128)S(1)}, s32[768,3,3]{0,2,1:T(4,128)}, u32[]{:S(2)}) copy-start(s32[768,3,3]{0,2,1:T(4,128)} %param.9) | copy-start | bytes 82948
  15.2 58.8 %collective-permute-start.10 = (bf16[384,1024]{1,0:T(8,128)(2,1)}, bf16[384,1024]{1,0:T(8,128)(2,1)}, u32[]{:S(2)}, u32[]{:S(2)}) collective-permute-start(bf16[384,1024]{1,0:T(8,128)(2,1)} %pad_maximum_fusion.3), channel_id=1, source_target_pairs={{16,0},{17,1},{18,2},{19,3},{20,4},{21,5},{22,6},{23,7},{24,8},{25... | collective-permute-start | bytes 2359304 | tf_op jit(solution)/shard_map/ppermute | solution.py:207
  22.6 17.0 %copy-start.6 = (bf16[384,1024]{1,0:T(8,128)(2,1)}, bf16[384,1024]{1,0:T(8,128)(2,1)S(1)}, u32[]{:S(2)}) copy-start(bf16[384,1024]{1,0:T(8,128)(2,1)S(1)} %collective-permute-done.2.nk.nv) | copy-start | bytes 2359300
  22.6 62.5 %collective-permute-start.8 = (bf16[384,1024]{1,0:T(8,128)(2,1)}, bf16[384,1024]{1,0:T(8,128)(2,1)}, u32[]{:S(2)}, u32[]{:S(2)}) collective-permute-start(bf16[384,1024]{1,0:T(8,128)(2,1)} %pad_maximum_fusion.3), channel_id=1, source_target_pairs={{1,0},{2,1},{3,2},{4,3},{5,4},{6,5},{7,6},{8,7},{9,8},{10,9},{11,1... | collective-permute-start | bytes 2359304 | tf_op jit(solution)/shard_map/ppermute | solution.py:207
  24.7 22.7 %copy-start = (bf16[384,1024]{1,0:T(8,128)(2,1)S(1)}, bf16[384,1024]{1,0:T(8,128)(2,1)}, u32[]{:S(2)}) copy-start(bf16[384,1024]{1,0:T(8,128)(2,1)} %k.11) | copy-start | bytes 2359300
  24.7 22.7 %copy-start.1 = (bf16[384,1024]{1,0:T(8,128)(2,1)S(1)}, bf16[384,1024]{1,0:T(8,128)(2,1)}, u32[]{:S(2)}) copy-start(bf16[384,1024]{1,0:T(8,128)(2,1)} %v.11) | copy-start | bytes 2359300
  25.7 0.9 copy-start.9
  26.6 99.2 %collective-permute-start.4 = (bf16[384,1024]{1,0:T(8,128)(2,1)}, bf16[384,1024]{1,0:T(8,128)(2,1)}, u32[]{:S(2)}, u32[]{:S(2)}) collective-permute-start(bf16[384,1024]{1,0:T(8,128)(2,1)} %pad_maximum_fusion.2), channel_id=1, source_target_pairs={{1,0},{2,1},{3,2},{4,3},{5,4},{6,5},{7,6},{8,7},{9,8},{10,9},{11,1... | collective-permute-start | bytes 2359304 | tf_op jit(solution)/shard_map/ppermute | solution.py:207
  39.6 0.9 copy-start.4
  40.5 85.3 %collective-permute-start.6 = (bf16[384,1024]{1,0:T(8,128)(2,1)}, bf16[384,1024]{1,0:T(8,128)(2,1)}, u32[]{:S(2)}, u32[]{:S(2)}) collective-permute-start(bf16[384,1024]{1,0:T(8,128)(2,1)} %pad_maximum_fusion.2), channel_id=1, source_target_pairs={{16,0},{17,1},{18,2},{19,3},{20,4},{21,5},{22,6},{23,7},{24,8},{25... | collective-permute-start | bytes 2359304 | tf_op jit(solution)/shard_map/ppermute | solution.py:207
  47.4 1.1 copy-start.7
  48.5 1.1 copy-start.10
  49.7 9.5 %copy-start.5 = (bf16[384,1024]{1,0:T(8,128)(2,1)S(1)}, bf16[384,1024]{1,0:T(8,128)(2,1)}, u32[]{:S(2)}) copy-start(bf16[384,1024]{1,0:T(8,128)(2,1)} %copy-done.4) | copy-start | bytes 2359300
  54.8 10.1 %copy-start.8 = (bf16[384,1024]{1,0:T(8,128)(2,1)S(1)}, bf16[384,1024]{1,0:T(8,128)(2,1)}, u32[]{:S(2)}) copy-start(bf16[384,1024]{1,0:T(8,128)(2,1)} %copy-done.6) | copy-start | bytes 2359300
  54.8 60.6 %collective-permute-start.11 = (f32[8,384]{1,0:T(8,128)S(1)}, f32[8,384]{1,0:T(8,128)S(1)}, u32[]{:S(2)}, u32[]{:S(2)}) collective-permute-start(f32[8,384]{1,0:T(8,128)S(1)} %stats.3), channel_id=1, source_target_pairs={{16,0},{17,1},{18,2},{19,3},{20,4},{21,5},{22,6},{23,7},{24,8},{25... | collective-permute-start | bytes 36872 | tf_op jit(solution)/shard_map/ppermute | solution.py:207
  74.0 43.9 %collective-permute-start.9 = (f32[8,384]{1,0:T(8,128)S(1)}, f32[8,384]{1,0:T(8,128)S(1)}, u32[]{:S(2)}, u32[]{:S(2)}) collective-permute-start(f32[8,384]{1,0:T(8,128)S(1)} %stats.3), channel_id=1, source_target_pairs={{1,0},{2,1},{3,2},{4,3},{5,4},{6,5},{7,6},{8,7},{9,8},{10,9},{11,1... | collective-permute-start | bytes 36872 | tf_op jit(solution)/shard_map/ppermute | solution.py:207
  85.2 40.7 %collective-permute-start.5 = (f32[8,384]{1,0:T(8,128)S(1)}, f32[8,384]{1,0:T(8,128)S(1)}, u32[]{:S(2)}, u32[]{:S(2)}) collective-permute-start(f32[8,384]{1,0:T(8,128)S(1)} %stats.2), channel_id=1, source_target_pairs={{1,0},{2,1},{3,2},{4,3},{5,4},{6,5},{7,6},{8,7},{9,8},{10,9},{11,1... | collective-permute-start | bytes 36872 | tf_op jit(solution)/shard_map/ppermute | solution.py:207
  115.4 10.4 %collective-permute-start.7 = (f32[8,384]{1,0:T(8,128)S(1)}, f32[8,384]{1,0:T(8,128)S(1)}, u32[]{:S(2)}, u32[]{:S(2)}) collective-permute-start(f32[8,384]{1,0:T(8,128)S(1)} %stats.2), channel_id=1, source_target_pairs={{16,0},{17,1},{18,2},{19,3},{20,4},{21,5},{22,6},{23,7},{24,8},{25... | collective-permute-start | bytes 36872 | tf_op jit(solution)/shard_map/ppermute | solution.py:207

commit v2 on v1

v2 whole, which is shorter than its diff:
```python
import functools
import math

import jax
import jax.numpy as jnp
from jax import lax
from jax.experimental import pallas as pl
from jax.experimental.pallas import tpu as pltpu
from jax.sharding import PartitionSpec as P

HEADS = 8
D = 128
PAGE = 128
PG = 3
TOK = PG * PAGE
AXES = ("inner", "outer")
MASKED = -1e30
SCALE = 1.0 / math.sqrt(D)
SCALE2 = SCALE * math.log2(math.e)
GROUPS = ((0, 4), (4, 4))
NT = (((1,), (1,)), ((), ()))
NN = (((1,), (0,)), ((), ()))
TN = (((0,), (0,)), ((), ()))


def dot(a, b, dims):
    return lax.dot_general(a, b, dims, preferred_element_type=jnp.float32)


def query_head(queries, cotangent, sources, biases):
    key_at = lax.broadcasted_iota(jnp.int32, (PAGE, PAGE), 0)
    causal = key_at <= lax.broadcasted_iota(jnp.int32, (PAGE, PAGE), 1)
    pages, tops, masses, moments = [], [], [], []
    for src, (keys, values) in enumerate(sources):
        scores, pushes = dot(keys, queries, NT), dot(values, cotangent, NT)
        for j in range(PG):
            lo = j * PAGE if src == 0 else 0
            rows = slice(j * PAGE, (j + 1) * PAGE)
            s, p = scores[rows, lo:], pushes[rows, lo:]
            if src == 0:
                diagonal = jnp.where(causal, s[:, :PAGE], MASKED)
                s = diagonal if j == PG - 1 else jnp.concatenate((diagonal, s[:, PAGE:]), axis=1)
            top = jnp.max(s, axis=0, keepdims=True)
            e = jnp.exp2((s - top) * SCALE2)
            mass = jnp.sum(e, axis=0, keepdims=True)
            moment = jnp.sum(e * p, axis=0, keepdims=True)
            top = top * SCALE2 + biases[3 * src + j : 3 * src + j + 1, lo:]
            if lo:
                zeros = jnp.zeros((1, lo), jnp.float32)
                top = jnp.concatenate((zeros + MASKED, top), axis=1)
                mass = jnp.concatenate((zeros, mass), axis=1)
                moment = jnp.concatenate((zeros, moment), axis=1)
            pages.append((e, p))
            tops.append(top)
            masses.append(mass)
            moments.append(moment)
    highest = functools.reduce(jnp.maximum, tops)
    factors = [jnp.exp2(top - highest) for top in tops]
    mass = functools.reduce(jnp.add, [f * m for f, m in zip(factors, masses)])
    moment = functools.reduce(jnp.add, [f * m for f, m in zip(factors, moments)])
    scale = 1.0 / mass
    correction = moment * scale
    grad_q = 0.0
    own = None
    for src, (keys, values) in enumerate(sources):
        probs, dscores = [], []
        for j in range(PG):
            lo = j * PAGE if src == 0 else 0
            e, p = pages[3 * src + j]
            prob = e * (factors[3 * src + j] * scale)[:, lo:]
            dscore = (prob * (p - correction[:, lo:])).astype(jnp.bfloat16)
            prob = prob.astype(jnp.bfloat16)
            if lo:
                zeros = jnp.zeros((PAGE, lo), jnp.bfloat16)
                dscore = jnp.concatenate((zeros, dscore), axis=1)
                prob = jnp.concatenate((zeros, prob), axis=1)
            dscores.append(dscore)
            probs.append(prob)
        dscore = jnp.concatenate(dscores, axis=0)
        if src == 0:
            own = (dot(dscore, queries, NN), dot(jnp.concatenate(probs, axis=0), cotangent, NN))
        grad_q = grad_q + dot(keys, dscore, TN)
    return highest + jnp.log2(mass), correction, (grad_q * SCALE).T, own


def pick(flag, usual, other, cols):
    return jnp.where(flag, other[:, cols], usual[:, cols])


def load(arrays, first, count, held, sems):
    cols = pl.ds(first * D, count * D)
    copies = [
        pltpu.make_async_copy(array.at[:, cols], held.at[n], sems.at[n])
        for n, array in enumerate(arrays)
    ]
    for copy in copies:
        copy.start()
    for copy in copies:
        copy.wait()
    return [held.at[n] for n in range(len(arrays))]


def query_kernel(first, count, flags, q, do, k, v, near, far, wrapped, bias, *rest):
    dq_out, stats, dk_out, dv_out, held, sems = rest[-6:]
    q, do, k, v = load((q, do, k, v), first, count, held, sems)
    biases = bias[...]
    totals, corrections = [], []
    for h in range(count):
        cols, second = slice(h * D, (h + 1) * D), slice((count + h) * D, (count + h + 1) * D)
        if wrapped is None:
            far_key, far_value = far[:, cols], far[:, second]
        else:
            use = flags[0] > 0
            far_key, far_value = pick(use, far, wrapped, cols), pick(use, far, wrapped, second)
        sources = ((k[:, cols], v[:, cols]), (near[:, cols], near[:, second]), (far_key, far_value))
        total, correction, grad_q, own = query_head(q[:, cols], do[:, cols], sources, biases)
        totals.append(total)
        corrections.append(correction)
        dq_out[:, cols] = grad_q.astype(dq_out.dtype)
        dk_out[:, cols], dv_out[:, cols] = own
    stats[...] = jnp.concatenate(totals + corrections, axis=0)


def spread(bias):
    rows = [jnp.broadcast_to(bias[j : j + 1], (PAGE, TOK)) for j in range(PG)]
    return jnp.concatenate(rows, axis=0)


def key_kernel(
    first, count, flags, k, v, own_dk, own_dv, near, near_stats, far, wrapped, far_stats, bias, *rest
):
    dk_out, dv_out, held, sems = rest[-4:]
    k, v = load((k, v), first, count, held, sems)
    biases = bias[...]
    for h in range(count):
        cols, second = slice(h * D, (h + 1) * D), slice((count + h) * D, (count + h + 1) * D)
        keys, values = k[:, cols], v[:, cols]
        grad_k, grad_v = own_dk[:, cols], own_dv[:, cols]
        if wrapped is None:
            far_pair = (far[:, cols], far[:, second])
        else:
            use = flags[1] > 0
            far_pair = (pick(use, far, wrapped, cols), pick(use, far, wrapped, second))
        pairs = ((near[:, cols], near[:, second]), far_pair)
        for src, ((queries, cotangent), stats) in enumerate(zip(pairs, (near_stats, far_stats))):
            total, correction = stats[h : h + 1], stats[count + h : count + h + 1]
            masks = spread(biases[9 + 3 * src : 12 + 3 * src])
            prob = jnp.exp2(dot(keys, queries, NT) * SCALE2 + masks - total)
            dscore = prob * (dot(values, cotangent, NT) - correction)
            grad_v = grad_v + dot(prob.astype(jnp.bfloat16), cotangent, NN)
            grad_k = grad_k + dot(dscore.astype(jnp.bfloat16), queries, NN)
        dk_out[:, cols] = (grad_k * SCALE).astype(dk_out.dtype)
        dv_out[:, cols] = grad_v.astype(dv_out.dtype)


def block(count, first):
    return pl.BlockSpec((TOK, count * D), lambda i: (0, first // count))


def whole(array):
    return pl.BlockSpec(array.shape, lambda i: (0, 0))


HBM = pl.BlockSpec(memory_space=pltpu.HBM)


def pack_kernel(first, count, k, v, q, do, key_value, query_cot, sems):
    cols = pl.ds(first * D, count * D)
    copies = []
    for n, (array, out, at) in enumerate(
        ((k, key_value, 0), (v, key_value, 1), (q, query_cot, 0), (do, query_cot, 1))
    ):
        to = out.at[:, pl.ds(at * count * D, count * D)]
        copies.append(pltpu.make_async_copy(array.at[:, cols], to, sems.at[n]))
    for copy in copies:
        copy.start()
    for copy in copies:
        copy.wait()


def pack(first, count, *arrays):
    shape = jax.ShapeDtypeStruct((TOK, 2 * count * D), jnp.bfloat16)
    return pl.pallas_call(
        functools.partial(pack_kernel, first, count),
        name="pack",
        in_specs=[HBM] * 4,
        out_specs=[pl.BlockSpec(memory_space=pltpu.VMEM)] * 2,
        out_shape=[shape, shape],
        scratch_shapes=[pltpu.SemaphoreType.DMA((4,))],
        cost_estimate=pl.CostEstimate(
            flops=0, bytes_accessed=16 * TOK * count * D, transcendentals=0
        ),
    )(*arrays)


def call(kernel, name, first, count, flags, ins, loaded, outs, carried, dots, pairs):
    held = [pair for pair in ins if pair is not None]
    present = [pair is not None for pair in ins]
    arrays = [flags] + [a for a, _ in held]
    in_specs = [pl.BlockSpec(memory_space=pltpu.SMEM)] + [s for _, s in held]
    aliases = {}
    for at, array in enumerate(carried):
        aliases[len(arrays)] = at
        arrays.append(array)
        in_specs.append(pl.BlockSpec(memory_space=pl.ANY))

    def run(flags_ref, *refs):
        refs = list(refs)
        given = [refs.pop(0) if here else None for here in present]
        kernel(first, count, flags_ref, *given, *refs)

    return pl.pallas_call(
        run,
        name=name,
        grid=(1,),
        in_specs=in_specs,
        out_specs=[s for _, s in outs],
        out_shape=[s for s, _ in outs],
        input_output_aliases=aliases,
        scratch_shapes=[
            pltpu.VMEM((loaded, TOK, count * D), jnp.bfloat16),
            pltpu.SemaphoreType.DMA((loaded,)),
        ],
        compiler_params=pltpu.CompilerParams(
            dimension_semantics=("arbitrary",), vmem_limit_bytes=48 * 1024 * 1024
        ),
        cost_estimate=pl.CostEstimate(
            flops=2 * dots * count * TOK * TOK * D,
            bytes_accessed=len(held) * count * TOK * D * 2,
            transcendentals=pairs * count * TOK * TOK,
        ),
    )(*arrays)


def biases_of(page_mask, block_at, block_count):
    def picked(at, source):
        part = lax.dynamic_slice(
            page_mask, (jnp.minimum(at, block_count - 1) * PG, source, 0), (PG, 1, PG)
        )[:, 0, :]
        return jnp.where(at < block_count, part, 0)

    parts = [picked(block_at, source) for source in range(3)]
    parts += [picked(block_at + 1, 1), picked(block_at + lax.axis_size("outer"), 2)]
    wide = jnp.concatenate([jnp.repeat(part, PAGE, axis=0) for part in parts], axis=1)
    wide = jnp.where(wide > 0, 0.0, MASKED).astype(jnp.float32)
    return jnp.concatenate((wide, wide[:, :1]), axis=1).T


def body(queries, key_rows, value_rows, cotangent, page_mask):
    n_inner, n_outer = lax.axis_size("inner"), lax.axis_size("outer")
    inner_at, outer_at = lax.axis_index("inner"), lax.axis_index("outer")
    block_at = inner_at * n_outer + outer_at
    span = n_inner // 2

    def at(i, o):
        return i * n_outer + o

    def back(pairs):
        return [(b, a) for a, b in pairs]

    spots = [(i, o) for i in range(n_inner) for o in range(n_outer)]
    near = [
        (at(i, o), at(i, o + 1) if o + 1 < n_outer else at((i + span) % n_inner, 0)) for i, o in spots
    ]
    ring = [(at(i, o), at(i // span * span + (i + 1) % span, o)) for i, o in spots]
    chain = [(at(i, o), at(i + 1, o)) for i, o in spots if i + 1 < n_inner]
    loop = [(at(i, o), at((i + 1) % n_inner, o)) for i, o in spots]
    hop = [(at(0, o), at(span, o)) for o in range(n_outer)]
    hop += [(at(n_inner - 1, o), at(span - 1, o)) for o in range(n_outer)]

    def send(array, pairs):
        return lax.ppermute(array, AXES, pairs)

    def after(array, *earlier):
        return lax.optimization_barrier((array,) + earlier)[0]

    local = (key_rows, value_rows, queries, cotangent)
    bias = biases_of(page_mask, block_at, n_inner * n_outer)
    flags = jnp.stack((inner_at == span, inner_at == span - 1)).astype(jnp.int32)
    kv0, qc0 = pack(*GROUPS[0], *local)
    near_kv0, near_qc0 = send(kv0, near), send(qc0, back(near))
    far_kv0, far_qc0 = send(kv0, chain), send(qc0, back(chain))
    kv1, qc1 = pack(*GROUPS[1], *local)
    near_kv1 = send(kv1, near)
    far_kv1, far_qc1 = send(kv1, ring), send(qc1, back(ring))
    wrapped = send(jnp.where(inner_at == 0, far_kv1, far_qc1), hop)
    near_qc1 = send(qc1, back(near))
    moved = [
        (near_kv0, near_qc0, far_kv0, far_qc0, None),
        (near_kv1, near_qc1, far_kv1, far_qc1, wrapped),
    ]

    out = jax.ShapeDtypeStruct((TOK, HEADS * D), jnp.bfloat16)
    grad_q, grad_k, grad_v = None, None, None
    for (first, count), (near_kv, near_qc, far_kv, far_qc, wrapped) in zip(GROUPS, moved):
        local = block(count, first)
        stats = jax.ShapeDtypeStruct((2 * count, TOK), jnp.float32)
        part = jax.ShapeDtypeStruct((TOK, count * D), jnp.float32)
        grad_q, stats, own_dk, own_dv = call(
            query_kernel, "query_side", first, count, flags,
            [
                (queries, HBM),
                (cotangent, HBM),
                (key_rows, HBM),
                (value_rows, HBM),
                (near_kv, whole(near_kv)),
                (far_kv, whole(far_kv)),
                None if wrapped is None else (wrapped, whole(wrapped)),
                (bias, whole(bias)),
            ],
            4,
            [(out, local), (stats, whole(stats)), (part, whole(part)), (part, whole(part))],
            [] if grad_q is None else [grad_q], 11, 3,
        )
        near_stats, far_stats = send(stats, back(near)), send(stats, back(loop))
        grad_k, grad_v = call(
            key_kernel, "key_side", first, count, flags,
            [
                (key_rows, HBM),
                (value_rows, HBM),
                (own_dk, whole(own_dk)),
                (own_dv, whole(own_dv)),
                (near_qc, whole(near_qc)),
                (near_stats, whole(near_stats)),
                (far_qc, whole(far_qc)),
                None if wrapped is None else (wrapped, whole(wrapped)),
                (far_stats, whole(far_stats)),
                (bias, whole(bias)),
            ],
            2,
            [(out, local), (out, local)],
            [] if grad_k is None else [grad_k, grad_v], 8, 2,
        )
    return (grad_q, grad_k, grad_v)


def solution(mesh):
    split = P(AXES, None)
    return jax.shard_map(
        body, mesh=mesh, in_specs=(split, split, split, split, P()),
        out_specs=(split, split, split), check_vma=False,
    )
```

time: 135 us -> 95.8 us (0.71)
  the two profiles are of different devices: /device:TPU:241 before, /device:TPU:1 now
where the time goes in v2:
time: 95.8 us; the launch traced here: 95.4 us
  waiting for transfers between devices  36.4 us (38%)
  Pallas kernels  29.5 us (31%)
  starting transfers between devices  25 us (26%)
  other arithmetic  3.04 us (3%)
  between operations  0.98 us (1%)
    ppermute x13, waiting for transfers between devices, send(): return lax.ppermute(array, AXES, pairs)  36.4 us
    ppermute x13, starting transfers between devices, send(): return lax.ppermute(array, AXES, pairs)  25 us
    pallas_call x4, Pallas kernels, call(): pl.pallas_call(run, name=name, grid=(1,), in_specs=in_specs, out_specs=[s...  24.4 us
    pallas_call x2, Pallas kernels, pack(): pl.pallas_call(functools.partial(pack_kernel, first, count), name='pack',...  5.16 us
    select_n x1, other arithmetic, body(): wrapped = send(jnp.where(inner_at == 0, far_kv1, far_qc1), hop)  2.1 us
  transfers between devices with their start and end apart: 13, of which 2 were waited for; matrix products, arithmetic and copies ran while one was open for 4% of the time, Pallas kernels for 23%

profile of v2, /device:TPU:1, one launch (start us, length us, event | category | flops | bytes accessed | tf_op | source)
XLA Modules:
  0.0 95.4 jit_solution(1795766942870485480)
XLA Ops:
  0.6 2.5 %pack.2 = (bf16[384,1024]{1,0:T(8,128)(2,1)}, bf16[384,1024]{1,0:T(8,128)(2,1)}) custom-call(bf16[384,1024]{1,0:T(8,128)(2,1)} %refs_0_.7, bf16[384,1024]{1,0:T(8,128)(2,1)} %refs_1_.7, bf16[384,1024]{1,0:T(8,128)(2,1)} %refs_0_.5, bf16[384,1024]{1,0:T(8,128)(2,1)} %refs_1_.5), custom_call_target="tpu_custom_call" | custom-call | bytes 3145728 | tf_op jit(solution)/shard_map/pack/pallas_call | solution.py:183
  3.2 2.6 %collective-permute-start.1 = (bf16[384,1024]{1,0:T(8,128)(2,1)}, bf16[384,1024]{1,0:T(8,128)(2,1)}, u32[]{:S(2)}, u32[]{:S(2)}) collective-permute-start(bf16[384,1024]{1,0:T(8,128)(2,1)} %get-tuple-element.19), channel_id=1, source_target_pairs={{0,16},{1,17},{2,18},{3,19},{4,20},{5,21},{6,22},{7,23},{8,24},{9,... | collective-permute-start | bytes 2359304 | tf_op jit(solution)/shard_map/ppermute | solution.py:272
  5.8 0.7 collective-permute-start.2
  6.5 0.0 copy-start.3
  6.5 2.6 %pack.3 = (bf16[384,1024]{1,0:T(8,128)(2,1)}, bf16[384,1024]{1,0:T(8,128)(2,1)}) custom-call(bf16[384,1024]{1,0:T(8,128)(2,1)} %refs_0_.7, bf16[384,1024]{1,0:T(8,128)(2,1)} %refs_1_.7, bf16[384,1024]{1,0:T(8,128)(2,1)} %refs_0_.5, bf16[384,1024]{1,0:T(8,128)(2,1)} %refs_1_.5), custom_call_target="tpu_custom_call" | custom-call | bytes 3145728 | tf_op jit(solution)/shard_map/pack/pallas_call | solution.py:183
  9.1 3.0 %collective-permute-start.5 = (bf16[384,1024]{1,0:T(8,128)(2,1)}, bf16[384,1024]{1,0:T(8,128)(2,1)}, u32[]{:S(2)}, u32[]{:S(2)}) collective-permute-start(bf16[384,1024]{1,0:T(8,128)(2,1)} %get-tuple-element.21), channel_id=1, source_target_pairs={{0,16},{1,17},{2,18},{3,19},{4,20},{5,21},{6,22},{7,23},{8,24},{9,... | collective-permute-start | bytes 2359304 | tf_op jit(solution)/shard_map/ppermute | solution.py:272
  12.1 1.4 %collective-permute-start.4 = (bf16[384,1024]{1,0:T(8,128)(2,1)}, bf16[384,1024]{1,0:T(8,128)(2,1)}, u32[]{:S(2)}, u32[]{:S(2)}) collective-permute-start(bf16[384,1024]{1,0:T(8,128)(2,1)} %get-tuple-element.21), channel_id=1, source_target_pairs={{0,1},{1,2},{2,3},{3,4},{4,5},{5,6},{6,7},{7,8},{8,9},{9,10},{10,1... | collective-permute-start | bytes 2359304 | tf_op jit(solution)/shard_map/ppermute | solution.py:272
  13.5 2.7 %collective-permute-start.11 = (bf16[384,1024]{1,0:T(8,128)(2,1)}, bf16[384,1024]{1,0:T(8,128)(2,1)}, u32[]{:S(2)}, u32[]{:S(2)}) collective-permute-start(bf16[384,1024]{1,0:T(8,128)(2,1)} %get-tuple-element.29), channel_id=1, source_target_pairs={{16,0},{17,1},{18,2},{19,3},{20,4},{21,5},{22,6},{23,7},{24,8},{25... | collective-permute-start | bytes 2359304 | tf_op jit(solution)/shard_map/ppermute | solution.py:272
  16.1 0.9 select_bitcast_fusion
  17.0 0.1 broadcast_bitcast_fusion
  17.1 0.1 broadcast_bitcast_fusion.2
  17.1 0.0 copy-start
  17.1 0.0 copy-start.1
  17.1 0.0 copy-start.2
  17.1 0.0 collective-permute-done.1.refs_5_
  17.2 6.2 %collective-permute-start.9 = (bf16[384,1024]{1,0:T(8,128)(2,1)}, bf16[384,1024]{1,0:T(8,128)(2,1)}, u32[]{:S(2)}, u32[]{:S(2)}) collective-permute-start(bf16[384,1024]{1,0:T(8,128)(2,1)} %get-tuple-element.29), channel_id=1, source_target_pairs={{1,0},{2,1},{3,2},{4,3},{5,4},{6,5},{7,6},{8,7},{9,8},{10,9},{11,1... | collective-permute-start | bytes 2359304 | tf_op jit(solution)/shard_map/ppermute | solution.py:272
  23.4 0.0 collective-permute-done.2.refs_6_
  23.4 0.0 collective-permute-start
  23.4 2.1 %broadcast_select_fusion = bf16[384,1024]{1,0:T(8,128)(2,1)} fusion(bf16[384,1024]{1,0:T(8,128)(2,1)} %collective-permute-done.1.refs_5_, bf16[384,1024]{1,0:T(8,128)(2,1)} %collective-permute-done.2.refs_6_, pred[]{:T(512)S(6)} %eq.11), kind=kLoop, calls=%fused_computation | loop fusion | flops 393216 | bytes 2359297 | tf_op jit(solution)/shard_map/jit(_where)/select_n | solution.py:286
  25.5 0.0 collective-permute-done.5.refs_5_
  25.5 1.6 %collective-permute-start.3 = (bf16[384,1024]{1,0:T(8,128)(2,1)}, bf16[384,1024]{1,0:T(8,128)(2,1)}, u32[]{:S(2)}, u32[]{:S(2)}) collective-permute-start(bf16[384,1024]{1,0:T(8,128)(2,1)} %broadcast_select_fusion), channel_id=1, source_target_pairs={{0,128},{1,129},{2,130},{3,131},{4,132},{5,133},{6,134},{7,135},{8... | collective-permute-start | bytes 2359304 | tf_op jit(solution)/shard_map/ppermute | solution.py:272
  27.0 0.1 broadcast_bitcast_fusion.4
  27.1 0.2 concatenate.6
  27.3 11.0 %collective-permute-done.4.refs_4_ = bf16[384,1024]{1,0:T(8,128)(2,1)} collective-permute-done((bf16[384,1024]{1,0:T(8,128)(2,1)}, bf16[384,1024]{1,0:T(8,128)(2,1)}, u32[]{:S(2)}, u32[]{:S(2)}) %collective-permute-start.4) | collective-permute-done | bytes 786464 | tf_op jit(solution)/shard_map/ppermute | solution.py:272
  38.3 1.2 %collective-permute-start.6 = (bf16[384,1024]{1,0:T(8,128)(2,1)}, bf16[384,1024]{1,0:T(8,128)(2,1)S(1)}, u32[]{:S(2)}, u32[]{:S(2)}) collective-permute-start(bf16[384,1024]{1,0:T(8,128)(2,1)} %get-tuple-element.20), channel_id=1, source_target_pairs={{1,0},{2,1},{3,2},{4,3},{5,4},{6,5},{7,6},{8,7},{9,8},{10,9},{11,1... | collective-permute-start | bytes 2359304 | tf_op jit(solution)/shard_map/ppermute | solution.py:272
  39.5 0.1 add_convert_fusion.flags_ref
  39.6 0.0 copy-done.3
  39.6 0.0 copy-done
  39.6 0.0 copy-done.1
  39.6 0.0 copy-done.2
  39.6 7.0 %query_side.2 = (bf16[384,1024]{1,0:T(8,128)(2,1)}, f32[8,384]{1,0:T(8,128)S(1)}, f32[384,512]{1,0:T(8,128)S(1)}, f32[384,512]{1,0:T(8,128)S(1)}) custom-call(s32[2]{0:T(128)S(1)} %add_convert_fusion.flags_ref, bf16[384,1024]{1,0:T(8,128)(2,1)S(1)} %copy-done.2, bf16[384,1024]{1,0:T(8,128)(2,1)S(1)} %copy-done.3, bf16[384,1024]{1,0:T(8,128)(2,1)S(1)} %copy-done, ...), custom_call_target="tpu_custom_call" | custom-call | flops 1660944384 | bytes 2752512 | tf_op jit(solution)/shard_map/query_side/pallas_call | solution.py:212
  46.6 25.4 %collective-permute-done.refs_4_ = bf16[384,1024]{1,0:T(8,128)(2,1)} collective-permute-done((bf16[384,1024]{1,0:T(8,128)(2,1)}, bf16[384,1024]{1,0:T(8,128)(2,1)}, u32[]{:S(2)}, u32[]{:S(2)}) %collective-permute-start) | collective-permute-done | bytes 786464 | tf_op jit(solution)/shard_map/ppermute | solution.py:272
  72.0 0.7 collective-permute-start.12
  72.7 0.0 collective-permute-done.3.refs_6_.refs_7_
  72.7 0.0 collective-permute-start.10
  72.7 7.3 %query_side.3 = (bf16[384,1024]{1,0:T(8,128)(2,1)}, f32[8,384]{1,0:T(8,128)S(1)}, f32[384,512]{1,0:T(8,128)S(1)}, f32[384,512]{1,0:T(8,128)S(1)}) custom-call(s32[2]{0:T(128)S(1)} %add_convert_fusion.flags_ref, bf16[384,1024]{1,0:T(8,128)(2,1)S(1)} %copy-done.2, bf16[384,1024]{1,0:T(8,128)(2,1)S(1)} %copy-done.3, ...), custom_call_target="tpu_custom_call", output_to_operand_aliasing={{0}: (9, {})} | custom-call | flops 1660944384 | bytes 3145728 | tf_op jit(solution)/shard_map/query_side/pallas_call | solution.py:212
  80.0 0.0 collective-permute-done.11.refs_6_
  80.0 5.0 %collective-permute-start.8 = (f32[8,384]{1,0:T(8,128)S(1)}, f32[8,384]{1,0:T(8,128)S(1)}, u32[]{:S(2)}, u32[]{:S(2)}) collective-permute-start(f32[8,384]{1,0:T(8,128)S(1)} %get-tuple-element.26), channel_id=1, source_target_pairs={{16,0},{17,1},{18,2},{19,3},{20,4},{21,5},{22,6},{23,7},{24,8},{25... | collective-permute-start | bytes 36872 | tf_op jit(solution)/shard_map/ppermute | solution.py:272
  85.1 0.0 collective-permute-done.9.refs_4_
  85.1 0.0 collective-permute-start.7
  85.1 0.0 collective-permute-done.12.refs_7_
  85.1 0.0 collective-permute-done.10.refs_5_
  85.1 5.0 %key_side.2 = (bf16[384,1024]{1,0:T(8,128)(2,1)}, bf16[384,1024]{1,0:T(8,128)(2,1)}) custom-call(s32[2]{0:T(128)S(1)} %add_convert_fusion.flags_ref, bf16[384,1024]{1,0:T(8,128)(2,1)S(1)} %copy-done, bf16[384,1024]{1,0:T(8,128)(2,1)S(1)} %copy-done.1, f32[384,512]{1,0:T(8,128)S(1)} %get-tuple-element.27.refs_2_, f32[384,512]{1,0:T(8,128)S(1)} %get-tuple-element.28.refs_3_, ...), custom_call_target="tpu_custom_call" | custom-call | flops 1207959552 | bytes 3538944 | tf_op jit(solution)/shard_map/key_side/pallas_call | solution.py:212
  90.1 0.0 collective-permute-done.6.refs_4_
  90.1 0.0 collective-permute-done.8.refs_8_
  90.1 0.0 collective-permute-done.7.refs_5_
  90.1 5.1 %key_side.3 = (bf16[384,1024]{1,0:T(8,128)(2,1)}, bf16[384,1024]{1,0:T(8,128)(2,1)}) custom-call(s32[2]{0:T(128)S(1)} %add_convert_fusion.flags_ref, bf16[384,1024]{1,0:T(8,128)(2,1)S(1)} %copy-done, bf16[384,1024]{1,0:T(8,128)(2,1)S(1)} %copy-done.1, f32[384,512]{1,0:T(8,128)S(1)} %get-tuple-element.24.refs_2_, ...), custom_call_target="tpu_custom_call", output_to_operand_aliasing={{0}: (11, {}), {1}: (12, {})} | custom-call | flops 1207959552 | bytes 3932160 | tf_op jit(solution)/shard_map/key_side/pallas_call | solution.py:212
  (8 shorter events, 0.0 us)
Async XLA Ops:
  3.2 14.0 %collective-permute-start.1 = (bf16[384,1024]{1,0:T(8,128)(2,1)}, bf16[384,1024]{1,0:T(8,128)(2,1)}, u32[]{:S(2)}, u32[]{:S(2)}) collective-permute-start(bf16[384,1024]{1,0:T(8,128)(2,1)} %get-tuple-element.19), channel_id=1, source_target_pairs={{0,16},{1,17},{2,18},{3,19},{4,20},{5,21},{6,22},{7,23},{8,24},{9,... | collective-permute-start | bytes 2359304 | tf_op jit(solution)/shard_map/ppermute | solution.py:272
  5.8 17.6 %collective-permute-start.2 = (bf16[384,1024]{1,0:T(8,128)(2,1)}, bf16[384,1024]{1,0:T(8,128)(2,1)}, u32[]{:S(2)}, u32[]{:S(2)}) collective-permute-start(bf16[384,1024]{1,0:T(8,128)(2,1)} %get-tuple-element.20), channel_id=1, source_target_pairs={{16,0},{17,1},{18,2},{19,3},{20,4},{21,5},{22,6},{23,7},{24,8},{25... | collective-permute-start | bytes 2359304 | tf_op jit(solution)/shard_map/ppermute | solution.py:272
  6.5 33.1 %copy-start.3 = (bf16[384,1024]{1,0:T(8,128)(2,1)S(1)}, bf16[384,1024]{1,0:T(8,128)(2,1)}, u32[]{:S(2)}) copy-start(bf16[384,1024]{1,0:T(8,128)(2,1)} %refs_1_.5) | copy-start | bytes 2359300
  9.1 16.4 %collective-permute-start.5 = (bf16[384,1024]{1,0:T(8,128)(2,1)}, bf16[384,1024]{1,0:T(8,128)(2,1)}, u32[]{:S(2)}, u32[]{:S(2)}) collective-permute-start(bf16[384,1024]{1,0:T(8,128)(2,1)} %get-tuple-element.21), channel_id=1, source_target_pairs={{0,16},{1,17},{2,18},{3,19},{4,20},{5,21},{6,22},{7,23},{8,24},{9,... | collective-permute-start | bytes 2359304 | tf_op jit(solution)/shard_map/ppermute | solution.py:272
  12.1 26.2 %collective-permute-start.4 = (bf16[384,1024]{1,0:T(8,128)(2,1)}, bf16[384,1024]{1,0:T(8,128)(2,1)}, u32[]{:S(2)}, u32[]{:S(2)}) collective-permute-start(bf16[384,1024]{1,0:T(8,128)(2,1)} %get-tuple-element.21), channel_id=1, source_target_pairs={{0,1},{1,2},{2,3},{3,4},{4,5},{5,6},{6,7},{7,8},{8,9},{9,10},{10,1... | collective-permute-start | bytes 2359304 | tf_op jit(solution)/shard_map/ppermute | solution.py:272
  13.5 66.6 %collective-permute-start.11 = (bf16[384,1024]{1,0:T(8,128)(2,1)}, bf16[384,1024]{1,0:T(8,128)(2,1)}, u32[]{:S(2)}, u32[]{:S(2)}) collective-permute-start(bf16[384,1024]{1,0:T(8,128)(2,1)} %get-tuple-element.29), channel_id=1, source_target_pairs={{16,0},{17,1},{18,2},{19,3},{20,4},{21,5},{22,6},{23,7},{24,8},{25... | collective-permute-start | bytes 2359304 | tf_op jit(solution)/shard_map/ppermute | solution.py:272
  17.1 22.5 %copy-start = (bf16[384,1024]{1,0:T(8,128)(2,1)S(1)}, bf16[384,1024]{1,0:T(8,128)(2,1)}, u32[]{:S(2)}) copy-start(bf16[384,1024]{1,0:T(8,128)(2,1)} %refs_0_.7) | copy-start | bytes 2359300
  17.1 22.5 %copy-start.1 = (bf16[384,1024]{1,0:T(8,128)(2,1)S(1)}, bf16[384,1024]{1,0:T(8,128)(2,1)}, u32[]{:S(2)}) copy-start(bf16[384,1024]{1,0:T(8,128)(2,1)} %refs_1_.7) | copy-start | bytes 2359300
  17.1 22.5 %copy-start.2 = (bf16[384,1024]{1,0:T(8,128)(2,1)S(1)}, bf16[384,1024]{1,0:T(8,128)(2,1)}, u32[]{:S(2)}) copy-start(bf16[384,1024]{1,0:T(8,128)(2,1)} %refs_0_.5) | copy-start | bytes 2359300
  17.2 67.9 %collective-permute-start.9 = (bf16[384,1024]{1,0:T(8,128)(2,1)}, bf16[384,1024]{1,0:T(8,128)(2,1)}, u32[]{:S(2)}, u32[]{:S(2)}) collective-permute-start(bf16[384,1024]{1,0:T(8,128)(2,1)} %get-tuple-element.29), channel_id=1, source_target_pairs={{1,0},{2,1},{3,2},{4,3},{5,4},{6,5},{7,6},{8,7},{9,8},{10,9},{11,1... | collective-permute-start | bytes 2359304 | tf_op jit(solution)/shard_map/ppermute | solution.py:272
  23.4 48.6 %collective-permute-start = (bf16[384,1024]{1,0:T(8,128)(2,1)}, bf16[384,1024]{1,0:T(8,128)(2,1)}, u32[]{:S(2)}, u32[]{:S(2)}) collective-permute-start(bf16[384,1024]{1,0:T(8,128)(2,1)} %get-tuple-element.19), channel_id=1, source_target_pairs={{0,1},{1,2},{2,3},{3,4},{4,5},{5,6},{6,7},{7,8},{8,9},{9,10},{10,1... | collective-permute-start | bytes 2359304 | tf_op jit(solution)/shard_map/ppermute | solution.py:272
  25.5 47.2 %collective-permute-start.3 = (bf16[384,1024]{1,0:T(8,128)(2,1)}, bf16[384,1024]{1,0:T(8,128)(2,1)}, u32[]{:S(2)}, u32[]{:S(2)}) collective-permute-start(bf16[384,1024]{1,0:T(8,128)(2,1)} %broadcast_select_fusion), channel_id=1, source_target_pairs={{0,128},{1,129},{2,130},{3,131},{4,132},{5,133},{6,134},{7,135},{8... | collective-permute-start | bytes 2359304 | tf_op jit(solution)/shard_map/ppermute | solution.py:272
  38.3 51.8 %collective-permute-start.6 = (bf16[384,1024]{1,0:T(8,128)(2,1)}, bf16[384,1024]{1,0:T(8,128)(2,1)S(1)}, u32[]{:S(2)}, u32[]{:S(2)}) collective-permute-start(bf16[384,1024]{1,0:T(8,128)(2,1)} %get-tuple-element.20), channel_id=1, source_target_pairs={{1,0},{2,1},{3,2},{4,3},{5,4},{6,5},{7,6},{8,7},{9,8},{10,9},{11,1... | collective-permute-start | bytes 2359304 | tf_op jit(solution)/shard_map/ppermute | solution.py:272
  72.0 13.1 %collective-permute-start.12 = (f32[8,384]{1,0:T(8,128)S(1)}, f32[8,384]{1,0:T(8,128)S(1)}, u32[]{:S(2)}, u32[]{:S(2)}) collective-permute-start(f32[8,384]{1,0:T(8,128)S(1)} %get-tuple-element.30), channel_id=1, source_target_pairs={{16,0},{17,1},{18,2},{19,3},{20,4},{21,5},{22,6},{23,7},{24,8},{25... | collective-permute-start | bytes 36872 | tf_op jit(solution)/shard_map/ppermute | solution.py:272
  72.7 12.4 %collective-permute-start.10 = (f32[8,384]{1,0:T(8,128)S(1)}, f32[8,384]{1,0:T(8,128)S(1)}, u32[]{:S(2)}, u32[]{:S(2)}) collective-permute-start(f32[8,384]{1,0:T(8,128)S(1)} %get-tuple-element.30), channel_id=1, source_target_pairs={{1,0},{2,1},{3,2},{4,3},{5,4},{6,5},{7,6},{8,7},{9,8},{10,9},{11,1... | collective-permute-start | bytes 36872 | tf_op jit(solution)/shard_map/ppermute | solution.py:272
  80.0 10.0 %collective-permute-start.8 = (f32[8,384]{1,0:T(8,128)S(1)}, f32[8,384]{1,0:T(8,128)S(1)}, u32[]{:S(2)}, u32[]{:S(2)}) collective-permute-start(f32[8,384]{1,0:T(8,128)S(1)} %get-tuple-element.26), channel_id=1, source_target_pairs={{16,0},{17,1},{18,2},{19,3},{20,4},{21,5},{22,6},{23,7},{24,8},{25... | collective-permute-start | bytes 36872 | tf_op jit(solution)/shard_map/ppermute | solution.py:272
  85.1 5.0 %collective-permute-start.7 = (f32[8,384]{1,0:T(8,128)S(1)}, f32[8,384]{1,0:T(8,128)S(1)}, u32[]{:S(2)}, u32[]{:S(2)}) collective-permute-start(f32[8,384]{1,0:T(8,128)S(1)} %get-tuple-element.26), channel_id=1, source_target_pairs={{1,0},{2,1},{3,2},{4,3},{5,4},{6,5},{7,6},{8,7},{9,8},{10,9},{11,1... | collective-permute-start | bytes 36872 | tf_op jit(solution)/shard_map/ppermute | solution.py:272

commit v3 on v2

v3 whole, which is shorter than its diff:
```python
import functools
import math

import jax
import jax.numpy as jnp
from jax import lax
from jax.experimental import pallas as pl
from jax.experimental.pallas import tpu as pltpu
from jax.sharding import PartitionSpec as P

HEADS = 8
ROW = 4
D = 128
PAGE = 128
PG = 3
TOK = PG * PAGE
AXES = ("inner", "outer")
MASKED = -1e30
SCALE = 1.0 / math.sqrt(D)
SCALE2 = SCALE * math.log2(math.e)
GROUPS = ((0, 4), (4, 4))
NT = (((1,), (1,)), ((), ()))
NN = (((1,), (0,)), ((), ()))
TN = (((0,), (0,)), ((), ()))


def dot(a, b, dims):
    return lax.dot_general(a, b, dims, preferred_element_type=jnp.float32)


def query_head(queries, cotangent, sources, masks):
    key_at = lax.broadcasted_iota(jnp.int32, (PAGE, PAGE), 0)
    causal = key_at <= lax.broadcasted_iota(jnp.int32, (PAGE, PAGE), 1)
    pages, tops, masses, moments = [], [], [], []
    for src, (keys, values) in enumerate(sources):
        scores, pushes = dot(keys, queries, NT), dot(values, cotangent, NT)
        for j in range(PG):
            lo = j * PAGE if src == 0 else 0
            rows = slice(j * PAGE, (j + 1) * PAGE)
            s, p = scores[rows, lo:], pushes[rows, lo:]
            if src == 0:
                diagonal = jnp.where(causal, s[:, :PAGE], MASKED)
                s = diagonal if j == PG - 1 else jnp.concatenate((diagonal, s[:, PAGE:]), axis=1)
            top = jnp.max(s, axis=0, keepdims=True)
            e = jnp.exp2((s - top) * SCALE2)
            mass = jnp.sum(e, axis=0, keepdims=True)
            moment = jnp.sum(e * p, axis=0, keepdims=True)
            top = top * SCALE2 + masks[3 * src + j][:, lo:]
            if lo:
                zeros = jnp.zeros((1, lo), jnp.float32)
                top = jnp.concatenate((zeros + MASKED, top), axis=1)
                mass = jnp.concatenate((zeros, mass), axis=1)
                moment = jnp.concatenate((zeros, moment), axis=1)
            pages.append((e, p))
            tops.append(top)
            masses.append(mass)
            moments.append(moment)
    highest = functools.reduce(jnp.maximum, tops)
    factors = [jnp.exp2(top - highest) for top in tops]
    mass = functools.reduce(jnp.add, [f * m for f, m in zip(factors, masses)])
    moment = functools.reduce(jnp.add, [f * m for f, m in zip(factors, moments)])
    scale = 1.0 / mass
    correction = moment * scale
    grad_q = 0.0
    own = None
    for src, (keys, values) in enumerate(sources):
        probs, dscores = [], []
        for j in range(PG):
            lo = j * PAGE if src == 0 else 0
            e, p = pages[3 * src + j]
            prob = e * (factors[3 * src + j] * scale)[:, lo:]
            dscore = (prob * (p - correction[:, lo:])).astype(jnp.bfloat16)
            prob = prob.astype(jnp.bfloat16)
            if lo:
                zeros = jnp.zeros((PAGE, lo), jnp.bfloat16)
                dscore = jnp.concatenate((zeros, dscore), axis=1)
                prob = jnp.concatenate((zeros, prob), axis=1)
            dscores.append(dscore)
            probs.append(prob)
        dscore = jnp.concatenate(dscores, axis=0)
        if src == 0:
            own = (dot(dscore, queries, NN), dot(jnp.concatenate(probs, axis=0), cotangent, NN))
        grad_q = grad_q + dot(keys, dscore, TN)
    return highest + jnp.log2(mass), correction, (grad_q * SCALE).T, own


def split(count, h):
    return slice(h * D, (h + 1) * D), slice((count + h) * D, (count + h + 1) * D)


def pair_of(use, usual, other, count, h):
    if other is None:
        return tuple(usual[:, at] for at in split(count, h))
    return tuple(jnp.where(use, other[:, at], usual[:, at]) for at in split(count, h))


def masks_of(flags, first):
    rows = []
    for j in range(PG):
        tiles = [
            jnp.full((1, PAGE), jnp.where(flags[first + i * PG + j] > 0, 0.0, MASKED), jnp.float32)
            for i in range(PG)
        ]
        rows.append(jnp.concatenate(tiles, axis=1))
    return rows


def query_kernel(first, count, flags, qc, kv, near, far, wrapped, *rest):
    last = first + count == HEADS
    if last:
        *earlier, stats, dk_out, dv_out, dq_whole, held, sem = rest
        dq_out = held
    else:
        stats, dk_out, dv_out, dq_out = rest
    at = first * D if last else 0
    masks = masks_of(flags, 2) + masks_of(flags, 11) + masks_of(flags, 20)
    totals, corrections = [], []
    for h in range(count):
        cols, second = split(count, h)
        sources = (
            (kv[:, cols], kv[:, second]),
            (near[:, cols], near[:, second]),
            pair_of(flags[0] > 0, far, wrapped, count, h),
        )
        total, correction, grad_q, own = query_head(qc[:, cols], qc[:, second], sources, masks)
        totals.append(total)
        corrections.append(correction)
        dq_out[:, at + h * D : at + (h + 1) * D] = grad_q.astype(dq_out.dtype)
        dk_out[:, cols], dv_out[:, cols] = own
    stats[...] = jnp.concatenate(totals + corrections, axis=0)
    if last:
        done = 0
        for part in earlier:
            held[:, done : done + part.shape[1]] = part[...]
            done += part.shape[1]
        copy = pltpu.make_async_copy(held, dq_whole, sem)
        copy.start()
        copy.wait()


def spread(rows):
    return jnp.concatenate([jnp.broadcast_to(row, (PAGE, TOK)) for row in rows], axis=0)


def key_head(keys, values, queries, cotangent, stats, count, h, mask):
    total, correction = stats[h : h + 1], stats[count + h : count + h + 1]
    prob = jnp.exp2(dot(keys, queries, NT) * SCALE2 + mask - total)
    dscore = prob * (dot(values, cotangent, NT) - correction)
    return (
        dot(dscore.astype(jnp.bfloat16), queries, NN), dot(prob.astype(jnp.bfloat16), cotangent, NN)
    )


def near_key_kernel(groups, flags, *refs):
    *refs, dk_out, dv_out = refs
    mask = spread(masks_of(flags, 29))
    for at, (first, count) in enumerate(groups):
        kv, own_dk, own_dv, near, stats = refs[5 * at : 5 * at + 5]
        for h in range(count):
            cols, second = split(count, h)
            grad_k, grad_v = key_head(
                kv[:, cols], kv[:, second], near[:, cols], near[:, second], stats, count, h, mask
            )
            to = slice((first + h) * D, (first + h + 1) * D)
            dk_out[:, to] = own_dk[:, cols] + grad_k
            dv_out[:, to] = own_dv[:, cols] + grad_v


def far_key_kernel(groups, flags, dk, dv, *rest):
    *refs, dk_whole, dv_whole, held, sems = rest
    mask = spread(masks_of(flags, 38))
    for at, (first, count) in enumerate(groups):
        kv, far, wrapped, stats = refs[4 * at : 4 * at + 4]
        for h in range(count):
            cols, second = split(count, h)
            grad_k, grad_v = key_head(
                kv[:, cols], kv[:, second], *pair_of(flags[1] > 0, far, wrapped, count, h),
                stats, count, h, mask,
            )
            to = slice((first + h) * D, (first + h + 1) * D)
            held[0, :, to] = ((dk[:, to] + grad_k) * SCALE).astype(held.dtype)
            held[1, :, to] = (dv[:, to] + grad_v).astype(held.dtype)
    copies = [
        pltpu.make_async_copy(held.at[n], whole, sems.at[n])
        for n, whole in enumerate((dk_whole, dv_whole))
    ]
    for copy in copies:
        copy.start()
    for copy in copies:
        copy.wait()


HBM = pl.BlockSpec(memory_space=pltpu.HBM)
VMEM = pl.BlockSpec(memory_space=pltpu.VMEM)


def pack(first, count, left, right):
    cols = slice(first * D, (first + count) * D)
    return jnp.concatenate((left[:, cols], right[:, cols]), axis=1)


def call(kernel, name, count, flags, ins, outs, scratch, dots, pairs):
    present = [array is not None for array in ins]
    arrays = [flags] + [array for array in ins if array is not None]

    def run(flags_ref, *refs):
        refs = list(refs)
        given = [refs.pop(0) if here else None for here in present]
        kernel(flags_ref, *given, *refs)

    return pl.pallas_call(
        run,
        name=name,
        in_specs=[pl.BlockSpec(memory_space=pltpu.SMEM)] + [VMEM] * (len(arrays) - 1),
        out_specs=[
            HBM if shape == jax.ShapeDtypeStruct((TOK, HEADS * D), jnp.bfloat16) else VMEM
            for shape in outs
        ],
        out_shape=outs,
        scratch_shapes=scratch,
        compiler_params=pltpu.CompilerParams(vmem_limit_bytes=40 * 1024 * 1024),
        cost_estimate=pl.CostEstimate(
            flops=2 * dots * count * TOK * TOK * D,
            bytes_accessed=len(ins) * count * TOK * D * 2,
            transcendentals=pairs * count * TOK * TOK,
        ),
    )(*arrays)


def flags_of(page_mask, wraps, block_at, block_count):
    def picked(at, source):
        part = lax.dynamic_slice(
            page_mask, (jnp.minimum(at, block_count - 1) * PG, source, 0), (PG, 1, PG)
        )
        return jnp.where(at < block_count, part, 0).reshape(PG * PG)

    parts = [picked(block_at, source) for source in range(3)]
    parts += [picked(block_at + 1, 1), picked(block_at + lax.axis_size("outer"), 2)]
    return jnp.concatenate([jnp.stack(wraps).astype(jnp.int32)] + parts)


def body(queries, key_rows, value_rows, cotangent, page_mask):
    n_inner, n_outer = lax.axis_size("inner"), lax.axis_size("outer")
    inner_at, outer_at = lax.axis_index("inner"), lax.axis_index("outer")
    block_at = inner_at * n_outer + outer_at
    span = n_inner // 2

    def at(i, o):
        return i * n_outer + o

    def back(pairs):
        return [(b, a) for a, b in pairs]

    spots = [(i, o) for i in range(n_inner) for o in range(n_outer)]
    near = [(at(i, o), at(i, o + 1)) for i, o in spots if o + 1 < n_outer]
    circle = [(at(i, o), at(i, (o + 1) % n_outer)) for i, o in spots]
    ring = [(at(i, o), at(i // span * span + (i + 1) % span, o)) for i, o in spots]
    loop = [(at(i, o), at((i + 1) % n_inner, o)) for i, o in spots]
    swap = [(at(span - 1, o), at(span, o)) for o in range(n_outer)]
    swap += back(swap)

    heights = 2 * n_outer // ROW

    def spot(end, z, y):
        z = z % heights
        half, low = z // (heights // 2), z % (heights // 2)
        return at(half * span + (span - 1 if end else 0), low * ROW + y)

    first_ring, first_back = ring[:], back(ring)
    for z in range(heights):
        old, new = (spot(1, z, ROW - 1), spot(0, z, ROW - 1)), spot(0, z - 1, ROW - 1)
        first_ring[first_ring.index(old)] = (old[0], new)
        old, new = (spot(0, z, ROW - 1), spot(1, z, ROW - 1)), spot(1, z - 1, ROW - 1)
        first_back[first_back.index(old)] = (old[0], new)
    hop = []
    for z in range(heights):
        upper = z >= heights // 2
        for y in range(ROW):
            relay = spot(upper, z - 1 if y == ROW - 1 else z, y)
            hop.append((relay, spot(upper, z - heights // 2, y)))

    def send(array, pairs):
        return lax.ppermute(array, AXES, pairs)

    def after(arrays):
        return lax.optimization_barrier(arrays)

    flags = flags_of(
        page_mask,
        (
            inner_at == span,
            inner_at == span - 1,
        ),
        block_at, n_inner * n_outer,
    )
    kv = [pack(*group, key_rows, value_rows) for group in GROUPS]
    qc = [pack(*group, queries, cotangent) for group in GROUPS]
    near0 = [send(kv[0], near), send(qc[0], back(near))]
    joint1 = [send(jnp.where(inner_at == span - 1, kv[1], qc[1]), swap)]
    far0 = [send(kv[0], first_ring), send(qc[0], first_back)]
    near1 = [send(kv[1], near)]
    joint0 = [send(jnp.where(inner_at % span == 0, far0[0], far0[1]), hop)]
    sides, far0 = after(((kv, qc), far0))
    far1 = [send(sides[0][1], ring), send(sides[1][1], back(ring))]
    later, near0 = after((qc[1], near0))
    near1.append(send(later, back(near)))
    near_kv, near_qc, far_kv, far_qc, wrapped = zip(near0 + far0 + joint0, near1 + far1 + joint1)

    grad_q, own, all_stats = [], [], []
    for turn, (first, count) in enumerate(GROUPS):
        last = first + count == HEADS
        stats = jax.ShapeDtypeStruct((2 * count, TOK), jnp.float32)
        part = jax.ShapeDtypeStruct((TOK, count * D), jnp.float32)
        out = jax.ShapeDtypeStruct((TOK, (HEADS if last else count) * D), jnp.bfloat16)
        held = [pltpu.VMEM(out.shape, out.dtype), pltpu.SemaphoreType.DMA] if last else []
        stats, own_dk, own_dv, grad = call(
            functools.partial(query_kernel, first, count), "query_side", count, flags,
            [qc[turn], kv[turn], near_kv[turn], far_kv[turn], wrapped[turn], *grad_q],
            [stats, part, part, out], held, 11, 3,
        )
        grad_q.append(grad)
        own.append((own_dk, own_dv))
        all_stats.append(stats)
    stats = jnp.concatenate(all_stats, axis=0)
    far_stats, near_stats = send(stats, back(loop)), send(stats, back(circle))
    ends = [2 * (first + count) for first, count in GROUPS]
    near_ins, far_ins = [], []
    for turn, (_, count) in enumerate(GROUPS):
        rows = slice(ends[turn] - 2 * count, ends[turn])
        near_ins += [kv[turn], *own[turn], near_qc[turn], near_stats[rows]]
        far_ins += [kv[turn], far_qc[turn], wrapped[turn], far_stats[rows]]
    sums = jax.ShapeDtypeStruct((TOK, HEADS * D), jnp.float32)
    dk, dv = call(
        functools.partial(near_key_kernel, GROUPS), "near_keys", HEADS, flags, near_ins,
        [sums, sums], [], 4, 1,
    )
    out = jax.ShapeDtypeStruct((TOK, HEADS * D), jnp.bfloat16)
    grad_k, grad_v = call(
        functools.partial(far_key_kernel, GROUPS), "far_keys", HEADS, flags, [dk, dv, *far_ins],
        [out, out],
        [pltpu.VMEM((2, *out.shape), out.dtype), pltpu.SemaphoreType.DMA((2,))], 4, 1,
    )
    return (grad_q[-1], grad_k, grad_v)


def solution(mesh):
    split = P(AXES, None)
    return jax.shard_map(
        body, mesh=mesh, in_specs=(split, split, split, split, P()),
        out_specs=(split, split, split), check_vma=False,
    )
```

time: 95.8 us -> 95.3 us (level)
  the two profiles are of different devices: /device:TPU:1 before, /device:TPU:7 now
where the time goes in v3:
time: 95.3 us; the launch traced here: 94.8 us
  starting transfers between devices  51.7 us (54%)
  Pallas kernels  23.8 us (25%)
  waiting for transfers between devices  8.19 us (9%)
  local copies, waits for them, and re-layouts  5.42 us (6%)
  other arithmetic  4.68 us (5%)
  between operations  0.96 us (1%)
    ppermute x12, starting transfers between devices, send(): return lax.ppermute(array, AXES, pairs)  51.7 us
    pallas_call x4, Pallas kernels, call(): pl.pallas_call(run, name=name, in_specs=[pl.BlockSpec(memory_space=pltpu....  23.8 us
    ppermute x12, waiting for transfers between devices, send(): return lax.ppermute(array, AXES, pairs)  8.19 us
    slice x2, local copies, waits for them, and re-layouts, pack(): return jnp.concatenate((left[:, cols], right[:, cols]), axis=1)  3.29 us
  transfers between devices with their start and end apart: 12, of which 5 were waited for; matrix products, arithmetic and copies ran while one was open for 6% of the time, Pallas kernels for 19%

profile of v3, /device:TPU:7, one launch (start us, length us, event | category | flops | bytes accessed | tf_op | source)
XLA Modules:
  0.0 94.8 jit_solution(13743451776352212711)
XLA Ops:
  0.6 2.3 %fusion = (bf16[384,512]{1,0:T(8,128)(2,1)S(1)}, bf16[384,512]{1,0:T(8,128)(2,1)S(1)}, bf16[384,512]{1,0:T(8,128)(2,1)}, bf16[384,512]{1,0:T(8,128)(2,1)S(1)}) fusion(bf16[384,1024]{1,0:T(8,128)(2,1)} %param.5, bf16[384,1024]{1,0:T(8,128)(2,1)} %param.8), kind=kLoop, calls=%fused_computation.14 | loop fusion | bytes 3145728 | tf_op jit(solution)/shard_map/slice | solution.py:199
  2.9 1.0 %pad_maximum_fusion.3.refs_0_ = bf16[384,1024]{1,0:T(8,128)(2,1)} fusion(bf16[384,512]{1,0:T(8,128)(2,1)S(1)} %get-tuple-element.62, bf16[384,512]{1,0:T(8,128)(2,1)S(1)} %get-tuple-element.44), kind=kLoop, calls=%fused_computation.3 | loop fusion | flops 1572864 | bytes 1572864 | tf_op jit(solution)/shard_map/concatenate | solution.py:199
  3.9 0.7 collective-permute-start.2
  4.6 1.0 %fusion.2 = (bf16[384,512]{1,0:T(8,128)(2,1)S(1)}, bf16[384,512]{1,0:T(8,128)(2,1)}, bf16[384,512]{1,0:T(8,128)(2,1)}, bf16[384,512]{1,0:T(8,128)(2,1)S(1)}) fusion(bf16[384,1024]{1,0:T(8,128)(2,1)S(1)} %copy-done.6, bf16[384,1024]{1,0:T(8,128)(2,1)S(1)} %copy-done.7), kind=kLoop, calls=%fused_computation.16 | loop fusion | bytes 3145728 | tf_op jit(solution)/shard_map/slice | solution.py:199
  5.6 0.1 pad_maximum_fusion.2.refs_1_.refs_0_.refs_2_
  5.7 2.5 %collective-permute-start.1 = (bf16[384,1024]{1,0:T(8,128)(2,1)S(1)}, bf16[384,1024]{1,0:T(8,128)(2,1)S(1)}, u32[]{:S(2)}, u32[]{:S(2)}) collective-permute-start(bf16[384,1024]{1,0:T(8,128)(2,1)S(1)} %pad_maximum_fusion.2.refs_1_.refs_0_.refs_2_), channel_id=1, source_target_pairs={{0,16},{1,17},{2,18},{3,19},{4,20},{5,21},{6,22},{7,23},{8,24},{9,... | collective-permute-start | bytes 2359304 | tf_op jit(solution)/shard_map/ppermute | solution.py:283
  8.2 1.3 %collective-permute-start.6 = (bf16[384,1024]{1,0:T(8,128)(2,1)}, bf16[384,1024]{1,0:T(8,128)(2,1)S(1)}, u32[]{:S(2)}, u32[]{:S(2)}) collective-permute-start(bf16[384,1024]{1,0:T(8,128)(2,1)} %pad_maximum_fusion.3.refs_0_), channel_id=1, source_target_pairs={{1,0},{2,1},{3,2},{4,3},{5,4},{6,5},{7,6},{8,7},{9,8},{10,9},{11,1... | collective-permute-start | bytes 2359304 | tf_op jit(solution)/shard_map/ppermute | solution.py:283
  9.5 4.9 %collective-permute-start.5 = (bf16[384,1024]{1,0:T(8,128)(2,1)S(1)}, bf16[384,1024]{1,0:T(8,128)(2,1)}, u32[]{:S(2)}, u32[]{:S(2)}) collective-permute-start(bf16[384,1024]{1,0:T(8,128)(2,1)S(1)} %pad_maximum_fusion.2.refs_1_.refs_0_.refs_2_), channel_id=1, source_target_pairs={{0,1},{1,2},{2,3},{3,4},{4,5},{5,6},{6,7},{7,8},{8,9},{9,10},{10,1... | collective-permute-start | bytes 2359304 | tf_op jit(solution)/shard_map/ppermute | solution.py:283
  14.4 2.3 %collective-permute-done.2.refs_3_ = bf16[384,1024]{1,0:T(8,128)(2,1)S(1)} collective-permute-done((bf16[384,1024]{1,0:T(8,128)(2,1)}, bf16[384,1024]{1,0:T(8,128)(2,1)S(1)}, u32[]{:S(2)}, u32[]{:S(2)}) %collective-permute-start.2) | collective-permute-done | bytes 786464 | tf_op jit(solution)/shard_map/ppermute | solution.py:283
  16.7 0.5 collective-permute-done.1.refs_3_
  17.2 1.1 %broadcast_select_fusion = bf16[384,1024]{1,0:T(8,128)(2,1)} fusion(bf16[384,1024]{1,0:T(8,128)(2,1)S(1)} %collective-permute-done.1.refs_3_, bf16[384,1024]{1,0:T(8,128)(2,1)S(1)} %collective-permute-done.2.refs_3_, pred[]{:T(512)S(6)} %eq.14), kind=kLoop, calls=%fused_computation.4 | loop fusion | flops 393216 | bytes 2359297 | tf_op jit(solution)/shard_map/jit(_where)/select_n | solution.py:302
  18.2 1.3 %collective-permute-start.7 = (bf16[384,1024]{1,0:T(8,128)(2,1)}, bf16[384,1024]{1,0:T(8,128)(2,1)}, u32[]{:S(2)}, u32[]{:S(2)}) collective-permute-start(bf16[384,1024]{1,0:T(8,128)(2,1)} %broadcast_select_fusion), channel_id=1, source_target_pairs={{0,128},{1,129},{2,130},{143,131},{4,132},{5,133},{6,134},{3,135},... | collective-permute-start | bytes 2359304 | tf_op jit(solution)/shard_map/ppermute | solution.py:283
  19.6 1.6 %broadcast_select_fusion.1 = (bf16[384,1024]{1,0:T(8,128)(2,1)}, bf16[384,1024]{1,0:T(8,128)(2,1)}, bf16[384,1024]{1,0:T(8,128)(2,1)S(1)}) fusion(pred[]{:T(512)} %eq.13, bf16[384,512]{1,0:T(8,128)(2,1)S(1)} %copy-done.5, bf16[384,512]{1,0:T(8,128)(2,1)S(1)} %copy-done.4, bf16[384,512]{1,0:T(8,128)(2,1)S(1)} %copy-done.3, ...), kind=kLoop, calls=%fused_computation.5 | loop fusion | flops 3538944 | bytes 3932161 | tf_op jit(solution)/shard_map/jit(_where)/select_n | solution.py:299
  21.2 12.0 %collective-permute-start.4 = (bf16[384,1024]{1,0:T(8,128)(2,1)}, bf16[384,1024]{1,0:T(8,128)(2,1)}, u32[]{:S(2)}, u32[]{:S(2)}) collective-permute-start(bf16[384,1024]{1,0:T(8,128)(2,1)} %get-tuple-element.41), channel_id=1, source_target_pairs={{112,128},{113,129},{114,130},{115,131},{116,132},{117,133},{118,1... | collective-permute-start | bytes 2359304 | tf_op jit(solution)/shard_map/ppermute | solution.py:283
  33.2 4.1 %collective-permute-start = (bf16[384,1024]{1,0:T(8,128)(2,1)S(1)}, bf16[384,1024]{1,0:T(8,128)(2,1)}, u32[]{:S(2)}, u32[]{:S(2)}) collective-permute-start(bf16[384,1024]{1,0:T(8,128)(2,1)S(1)} %get-tuple-element.22.refs_1_.refs_5_.refs_6_), channel_id=1, source_target_pairs={{0,1},{1,2},{2,3},{3,4},{4,5},{5,6},{6,7},{7,8},{8,9},{9,10},{10,1... | collective-permute-start | bytes 2359304 | tf_op jit(solution)/shard_map/ppermute | solution.py:283
  37.3 0.0 collective-permute-done.6.refs_3_
  37.3 2.0 %collective-permute-start.3 = (bf16[384,1024]{1,0:T(8,128)(2,1)S(1)}, bf16[384,1024]{1,0:T(8,128)(2,1)}, u32[]{:S(2)}, u32[]{:S(2)}) collective-permute-start(bf16[384,1024]{1,0:T(8,128)(2,1)S(1)} %get-tuple-element.22.refs_1_.refs_5_.refs_6_), channel_id=1, source_target_pairs={{0,16},{1,17},{2,18},{3,19},{4,20},{5,21},{6,22},{7,23},{8,24},{9,... | collective-permute-start | bytes 2359304 | tf_op jit(solution)/shard_map/ppermute | solution.py:283
  39.3 0.8 dynamic-slice_select_fusion
  40.2 0.1 copy.17
  40.3 0.1 reshape.25
  40.4 0.1 copy.15
  40.5 0.1 reshape.23
  40.5 0.1 copy.14
  40.6 0.1 reshape.22
  40.7 0.1 copy.13
  40.8 0.1 add_convert_fusion
  40.9 0.0 collective-permute-done.5.refs_2_
  40.9 1.5 %collective-permute-start.9 = (bf16[384,1024]{1,0:T(8,128)(2,1)}, bf16[384,1024]{1,0:T(8,128)(2,1)}, u32[]{:S(2)}, u32[]{:S(2)}) collective-permute-start(bf16[384,1024]{1,0:T(8,128)(2,1)} %get-tuple-element.38.refs_0_), channel_id=1, source_target_pairs={{1,0},{2,1},{3,2},{4,3},{5,4},{6,5},{7,6},{8,7},{9,8},{10,9},{11,1... | collective-permute-start | bytes 2359304 | tf_op jit(solution)/shard_map/ppermute | solution.py:283
  42.4 0.1 reshape.21
  42.4 0.1 copy.16
  42.5 0.1 reshape.24
  42.6 0.1 concatenate.18.flags_ref
  42.7 0.0 collective-permute-done.7.refs_4_
  42.7 0.0 collective-permute-start.11
  42.7 1.1 %copy-done.1 = bf16[384,1024]{1,0:T(8,128)(2,1)S(1)} copy-done((bf16[384,1024]{1,0:T(8,128)(2,1)S(1)}, bf16[384,1024]{1,0:T(8,128)(2,1)}, u32[]{:S(2)}) %copy-start.1) | copy-done | bytes 786456
  43.9 6.5 %query_side.2 = (f32[8,384]{1,0:T(8,128)S(1)}, f32[384,512]{1,0:T(8,128)S(1)}, f32[384,512]{1,0:T(8,128)S(1)}, bf16[384,512]{1,0:T(8,128)(2,1)S(1)}) custom-call(s32[47]{0:T(128)S(1)} %concatenate.18.flags_ref, bf16[384,1024]{1,0:T(8,128)(2,1)} %pad_maximum_fusion.3.refs_0_, bf16[384,1024]{1,0:T(8,128)(2,1)S(1)} %pad_maximum_fusion.2.refs_1_.refs_0_.refs_2_, ...), custom_call_target="tpu_custom_call" | custom-call | flops 1660944384 | bytes 1966080 | tf_op jit(solution)/shard_map/query_side/pallas_call | solution.py:211
  50.4 0.4 collective-permute-done.4.refs_4_.refs_8_
  50.8 0.0 collective-permute-done.refs_2_
  50.8 0.0 collective-permute-done.3.refs_3_
  50.8 7.3 %query_side.3 = (f32[8,384]{1,0:T(8,128)S(1)}, f32[384,512]{1,0:T(8,128)S(1)}, f32[384,512]{1,0:T(8,128)S(1)}, bf16[384,1024]{1,0:T(8,128)(2,1)}) custom-call(s32[47]{0:T(128)S(1)} %concatenate.18.flags_ref, bf16[384,1024]{1,0:T(8,128)(2,1)S(1)} %copy-done.2, bf16[384,1024]{1,0:T(8,128)(2,1)S(1)} %get-tuple-element.22.refs_1_.refs_5_.refs_6_, ...), custom_call_target="tpu_custom_call" | custom-call | flops 1660944384 | bytes 2359296 | tf_op jit(solution)/shard_map/query_side/pallas_call | solution.py:211
  58.1 21.5 %collective-permute-start.8 = (f32[16,384]{1,0:T(8,128)S(1)}, f32[16,384]{1,0:T(8,128)S(1)}, u32[]{:S(2)}, u32[]{:S(2)}) collective-permute-start(f32[16,384]{1,0:T(8,128)S(1)} %constant_dynamic-update-slice_fusion), channel_id=1, source_target_pairs={{1,0},{2,1},{3,2},{4,3},{5,4},{6,5},{7,6},{8,7},{9,8},{10,9},{11,1... | collective-permute-start | bytes 73736 | tf_op jit(solution)/shard_map/ppermute | solution.py:283
  79.6 0.0 collective-permute-start.10
  79.6 0.9 collective-permute-done.8
  80.5 0.0 collective-permute-done.9.refs_8_
  80.5 4.3 %near_keys.1 = (f32[384,1024]{1,0:T(8,128)S(1)}, f32[384,1024]{1,0:T(8,128)S(1)}) custom-call(s32[47]{0:T(128)S(1)} %concatenate.18.flags_ref, bf16[384,1024]{1,0:T(8,128)(2,1)S(1)} %pad_maximum_fusion.2.refs_1_.refs_0_.refs_2_, f32[384,512]{1,0:T(8,128)S(1)} %get-tuple-element.27.refs_1_, f32[384,512]{1,0:T(8,128)S(1)} %get-tuple-element.28.refs_2_, ...), custom_call_target="tpu_custom_call" | custom-call | flops 1207959552 | bytes 7864320 | tf_op jit(solution)/shard_map/near_keys/pallas_call | solution.py:211
  84.8 4.0 %collective-permute-done.10 = f32[16,384]{1,0:T(8,128)S(1)} collective-permute-done((f32[16,384]{1,0:T(8,128)S(1)}, f32[16,384]{1,0:T(8,128)S(1)}, u32[]{:S(2)}, u32[]{:S(2)}) %collective-permute-start.10) | collective-permute-done | bytes 24608 | tf_op jit(solution)/shard_map/ppermute | solution.py:283
  88.8 0.0 collective-permute-done.11.refs_7_
  88.8 5.8 %far_keys.1 = (bf16[384,1024]{1,0:T(8,128)(2,1)}, bf16[384,1024]{1,0:T(8,128)(2,1)}) custom-call(s32[47]{0:T(128)S(1)} %concatenate.18.flags_ref, f32[384,1024]{1,0:T(8,128)S(1)} %get-tuple-element.35.refs_0_, f32[384,1024]{1,0:T(8,128)S(1)} %get-tuple-element.36.refs_1_, bf16[384,1024]{1,0:T(8,128)(2,1)S(1)} %pad_maximum_fusion.2.refs_1_.refs_0_.refs_2_, ...), custom_call_target="tpu_custom_call" | custom-call | flops 1207959552 | bytes 7864320 | tf_op jit(solution)/shard_map/far_keys/pallas_call | solution.py:211
  (19 shorter events, 0.0 us)
Async XLA Ops:
  2.9 1.7 %copy-start.6 = (bf16[384,1024]{1,0:T(8,128)(2,1)S(1)}, bf16[384,1024]{1,0:T(8,128)(2,1)}, u32[]{:S(2)}) copy-start(bf16[384,1024]{1,0:T(8,128)(2,1)} %param.6) | copy-start | bytes 2359300
  2.9 1.7 %copy-start.7 = (bf16[384,1024]{1,0:T(8,128)(2,1)S(1)}, bf16[384,1024]{1,0:T(8,128)(2,1)}, u32[]{:S(2)}) copy-start(bf16[384,1024]{1,0:T(8,128)(2,1)} %param.7) | copy-start | bytes 2359300
  3.9 12.8 %collective-permute-start.2 = (bf16[384,1024]{1,0:T(8,128)(2,1)}, bf16[384,1024]{1,0:T(8,128)(2,1)S(1)}, u32[]{:S(2)}, u32[]{:S(2)}) collective-permute-start(bf16[384,1024]{1,0:T(8,128)(2,1)} %pad_maximum_fusion.3.refs_0_), channel_id=1, source_target_pairs={{16,0},{17,1},{18,2},{19,3},{20,4},{21,5},{22,6},{23,7},{24,8},{25... | collective-permute-start | bytes 2359304 | tf_op jit(solution)/shard_map/ppermute | solution.py:283
  5.7 11.5 %collective-permute-start.1 = (bf16[384,1024]{1,0:T(8,128)(2,1)S(1)}, bf16[384,1024]{1,0:T(8,128)(2,1)S(1)}, u32[]{:S(2)}, u32[]{:S(2)}) collective-permute-start(bf16[384,1024]{1,0:T(8,128)(2,1)S(1)} %pad_maximum_fusion.2.refs_1_.refs_0_.refs_2_), channel_id=1, source_target_pairs={{0,16},{1,17},{2,18},{3,19},{4,20},{5,21},{6,22},{7,23},{8,24},{9,... | collective-permute-start | bytes 2359304 | tf_op jit(solution)/shard_map/ppermute | solution.py:283
  8.2 29.1 %collective-permute-start.6 = (bf16[384,1024]{1,0:T(8,128)(2,1)}, bf16[384,1024]{1,0:T(8,128)(2,1)S(1)}, u32[]{:S(2)}, u32[]{:S(2)}) collective-permute-start(bf16[384,1024]{1,0:T(8,128)(2,1)} %pad_maximum_fusion.3.refs_0_), channel_id=1, source_target_pairs={{1,0},{2,1},{3,2},{4,3},{5,4},{6,5},{7,6},{8,7},{9,8},{10,9},{11,1... | collective-permute-start | bytes 2359304 | tf_op jit(solution)/shard_map/ppermute | solution.py:283
  9.5 31.3 %collective-permute-start.5 = (bf16[384,1024]{1,0:T(8,128)(2,1)S(1)}, bf16[384,1024]{1,0:T(8,128)(2,1)}, u32[]{:S(2)}, u32[]{:S(2)}) collective-permute-start(bf16[384,1024]{1,0:T(8,128)(2,1)S(1)} %pad_maximum_fusion.2.refs_1_.refs_0_.refs_2_), channel_id=1, source_target_pairs={{0,1},{1,2},{2,3},{3,4},{4,5},{5,6},{6,7},{7,8},{8,9},{9,10},{10,1... | collective-permute-start | bytes 2359304 | tf_op jit(solution)/shard_map/ppermute | solution.py:283
  14.4 5.1 %copy-start.3 = (bf16[384,512]{1,0:T(8,128)(2,1)S(1)}, bf16[384,512]{1,0:T(8,128)(2,1)}, u32[]{:S(2)}) copy-start(bf16[384,512]{1,0:T(8,128)(2,1)} %get-tuple-element.61) | copy-start | bytes 1179652
  14.4 5.1 %copy-start.4 = (bf16[384,512]{1,0:T(8,128)(2,1)S(1)}, bf16[384,512]{1,0:T(8,128)(2,1)}, u32[]{:S(2)}) copy-start(bf16[384,512]{1,0:T(8,128)(2,1)} %get-tuple-element.49) | copy-start | bytes 1179652
  14.4 5.1 %copy-start.5 = (bf16[384,512]{1,0:T(8,128)(2,1)S(1)}, bf16[384,512]{1,0:T(8,128)(2,1)}, u32[]{:S(2)}) copy-start(bf16[384,512]{1,0:T(8,128)(2,1)} %get-tuple-element.63) | copy-start | bytes 1179652
  17.2 2.4 %copy-start = (bf16[384,1024]{1,0:T(8,128)(2,1)}, bf16[384,1024]{1,0:T(8,128)(2,1)S(1)}, u32[]{:S(2)}) copy-start(bf16[384,1024]{1,0:T(8,128)(2,1)S(1)} %collective-permute-done.1.refs_3_) | copy-start | bytes 2359300
  18.2 24.5 %collective-permute-start.7 = (bf16[384,1024]{1,0:T(8,128)(2,1)}, bf16[384,1024]{1,0:T(8,128)(2,1)}, u32[]{:S(2)}, u32[]{:S(2)}) collective-permute-start(bf16[384,1024]{1,0:T(8,128)(2,1)} %broadcast_select_fusion), channel_id=1, source_target_pairs={{0,128},{1,129},{2,130},{143,131},{4,132},{5,133},{6,134},{3,135},... | collective-permute-start | bytes 2359304 | tf_op jit(solution)/shard_map/ppermute | solution.py:283
  21.2 29.6 %collective-permute-start.4 = (bf16[384,1024]{1,0:T(8,128)(2,1)}, bf16[384,1024]{1,0:T(8,128)(2,1)}, u32[]{:S(2)}, u32[]{:S(2)}) collective-permute-start(bf16[384,1024]{1,0:T(8,128)(2,1)} %get-tuple-element.41), channel_id=1, source_target_pairs={{112,128},{113,129},{114,130},{115,131},{116,132},{117,133},{118,1... | collective-permute-start | bytes 2359304 | tf_op jit(solution)/shard_map/ppermute | solution.py:283
  33.2 17.6 %collective-permute-start = (bf16[384,1024]{1,0:T(8,128)(2,1)S(1)}, bf16[384,1024]{1,0:T(8,128)(2,1)}, u32[]{:S(2)}, u32[]{:S(2)}) collective-permute-start(bf16[384,1024]{1,0:T(8,128)(2,1)S(1)} %get-tuple-element.22.refs_1_.refs_5_.refs_6_), channel_id=1, source_target_pairs={{0,1},{1,2},{2,3},{3,4},{4,5},{5,6},{6,7},{7,8},{8,9},{9,10},{10,1... | collective-permute-start | bytes 2359304 | tf_op jit(solution)/shard_map/ppermute | solution.py:283
  37.3 13.5 %collective-permute-start.3 = (bf16[384,1024]{1,0:T(8,128)(2,1)S(1)}, bf16[384,1024]{1,0:T(8,128)(2,1)}, u32[]{:S(2)}, u32[]{:S(2)}) collective-permute-start(bf16[384,1024]{1,0:T(8,128)(2,1)S(1)} %get-tuple-element.22.refs_1_.refs_5_.refs_6_), channel_id=1, source_target_pairs={{0,16},{1,17},{2,18},{3,19},{4,20},{5,21},{6,22},{7,23},{8,24},{9,... | collective-permute-start | bytes 2359304 | tf_op jit(solution)/shard_map/ppermute | solution.py:283
  40.9 39.6 %collective-permute-start.9 = (bf16[384,1024]{1,0:T(8,128)(2,1)}, bf16[384,1024]{1,0:T(8,128)(2,1)}, u32[]{:S(2)}, u32[]{:S(2)}) collective-permute-start(bf16[384,1024]{1,0:T(8,128)(2,1)} %get-tuple-element.38.refs_0_), channel_id=1, source_target_pairs={{1,0},{2,1},{3,2},{4,3},{5,4},{6,5},{7,6},{8,7},{9,8},{10,9},{11,1... | collective-permute-start | bytes 2359304 | tf_op jit(solution)/shard_map/ppermute | solution.py:283
  42.7 46.1 %collective-permute-start.11 = (bf16[384,1024]{1,0:T(8,128)(2,1)}, bf16[384,1024]{1,0:T(8,128)(2,1)S(1)}, u32[]{:S(2)}, u32[]{:S(2)}) collective-permute-start(bf16[384,1024]{1,0:T(8,128)(2,1)} %get-tuple-element.38.refs_0_), channel_id=1, source_target_pairs={{16,0},{17,1},{18,2},{19,3},{20,4},{21,5},{22,6},{23,7},{24,8},{25... | collective-permute-start | bytes 2359304 | tf_op jit(solution)/shard_map/ppermute | solution.py:283
  42.7 1.1 %copy-start.1 = (bf16[384,1024]{1,0:T(8,128)(2,1)S(1)}, bf16[384,1024]{1,0:T(8,128)(2,1)}, u32[]{:S(2)}) copy-start(bf16[384,1024]{1,0:T(8,128)(2,1)} %copy-done) | copy-start | bytes 2359300
  43.9 6.9 %copy-start.2 = (bf16[384,1024]{1,0:T(8,128)(2,1)S(1)}, bf16[384,1024]{1,0:T(8,128)(2,1)}, u32[]{:S(2)}) copy-start(bf16[384,1024]{1,0:T(8,128)(2,1)} %get-tuple-element.38.refs_0_) | copy-start | bytes 2359300
  58.1 22.4 %collective-permute-start.8 = (f32[16,384]{1,0:T(8,128)S(1)}, f32[16,384]{1,0:T(8,128)S(1)}, u32[]{:S(2)}, u32[]{:S(2)}) collective-permute-start(f32[16,384]{1,0:T(8,128)S(1)} %constant_dynamic-update-slice_fusion), channel_id=1, source_target_pairs={{1,0},{2,1},{3,2},{4,3},{5,4},{6,5},{7,6},{8,7},{9,8},{10,9},{11,1... | collective-permute-start | bytes 73736 | tf_op jit(solution)/shard_map/ppermute | solution.py:283
  79.6 9.3 %collective-permute-start.10 = (f32[16,384]{1,0:T(8,128)S(1)}, f32[16,384]{1,0:T(8,128)S(1)}, u32[]{:S(2)}, u32[]{:S(2)}) collective-permute-start(f32[16,384]{1,0:T(8,128)S(1)} %constant_dynamic-update-slice_fusion), channel_id=1, source_target_pairs={{16,0},{17,1},{18,2},{19,3},{20,4},{21,5},{22,6},{23,7},{24,8},{25... | collective-permute-start | bytes 73736 | tf_op jit(solution)/shard_map/ppermute | solution.py:283
